TPU v7x, 128 devices: a whole 4x4x4 slice. The times are simulated.
128 devices in a mesh: section: 2 (over x_hi), dp: 16 (over y, x_lo, core), tensor: 4 (over z).
Axes of the slice: x: 4 (x_hi: 2, x_lo: 2; x = x_hi * 2 + x_lo), y: 4, z: 4, core: 2. Of those that a mesh axis runs over, the one named last changes fastest.
Arguments:
- inputs: bfloat16 [2, 16, 256, 2048], P(None, 'dp', 'tensor'), may hold values from -6 to 6
- cotangent: bfloat16 [2, 16, 256, 2048], P(None, 'dp', 'tensor'), may hold values from -6 to 6
- doc_split: int32 [2, 16], P(None, 'dp'), may hold values from 16 to 240, as said below
- qkv_weight: bfloat16 [2, 2048, 3, 2048], P('section', 'dp', None, 'tensor'), may hold values from -0.125 to 0.125
- qkv_bias: float32 [2, 3, 2048], P('section', None, 'tensor'), may hold values from -3 to 3
- out_weight: bfloat16 [2, 2048, 2048], P('section', 'tensor', 'dp'), may hold values from -0.5 to 0.5
- out_bias: float32 [2, 2048], P('section'), may hold values from -2 to 2
- fc1_weight: bfloat16 [2, 2048, 8192], P('section', 'dp', 'tensor'), may hold values from -0.125 to 0.125
- fc1_bias: float32 [2, 8192], P('section', 'tensor'), may hold values from -3 to 3
- fc2_weight: bfloat16 [2, 8192, 2048], P('section', 'tensor', 'dp'), may hold values from -0.0625 to 0.0625
- fc2_bias: float32 [2, 2048], P('section'), may hold values from -2 to 2
- ln_gain: float32 [2, 2048], P('section'), may hold values from 0.5 to 1.5
- ln_bias: float32 [2, 2048], P('section'), may hold values from -2 to 2
Outputs:
- layer_out: bfloat16 [2, 2, 16, 256, 2048], P('section', None, 'dp', 'tensor')
- input_grad: bfloat16 [2, 2, 16, 256, 2048], P('section', None, 'dp', 'tensor')
- grad_qkv_weight: float32 [2, 2048, 3, 2048], P('section', 'dp', None, 'tensor')
- grad_qkv_bias: float32 [2, 3, 2048], P('section', None, 'tensor')
- grad_out_weight: float32 [2, 2048, 2048], P('section', 'tensor', 'dp')
- grad_out_bias: float32 [2, 2048], P('section')
- grad_fc1_weight: float32 [2, 2048, 8192], P('section', 'dp', 'tensor')
- grad_fc1_bias: float32 [2, 8192], P('section', 'tensor')
- grad_fc2_weight: float32 [2, 8192, 2048], P('section', 'tensor', 'dp')
- grad_fc2_bias: float32 [2, 2048], P('section')
- grad_ln_gain: float32 [2, 2048], P('section')
- grad_ln_bias: float32 [2, 2048], P('section')
Inputs may be any that keep to these rules, and one draw needn't show every extreme that they name: `doc_split`: each entry is at most 63 or at least 193; the first document of its slot has that many rows and the second the rest.
All inputs are finite; a program needn't handle non-finite values.
Results may differ from a plain program's by a relative error of at most 0.035.
Values may be sent and summed in bfloat16 or wider, within the bound.
A program may use at most 192 MiB of HBM per device.

v0:
```python
from functools import partial

import jax
import jax.numpy as jnp
from jax import lax
from jax.sharding import PartitionSpec as P

HD = 64
ROT = 32


EPSILON = 1e-05


def from_behind(array, axis, by):
    peers = lax.axis_size(axis)
    pairs = [(i, i + by) for i in range(peers) if 0 <= i + by < peers]
    return lax.ppermute(array, axis, pairs)


def layer_norm(values_in, norm_gain, shift_term):
    average = jnp.mean(values_in, axis=-1, keepdims=True)
    centred = values_in - average
    variance = jnp.mean(centred * centred, axis=-1, keepdims=True)
    return centred * lax.rsqrt(variance + EPSILON) * norm_gain + shift_term


def doc_layout(split_at, count):
    places = jnp.arange(count, dtype=jnp.int32)
    leading = places < split_at
    positions = jnp.where(leading, places, places - split_at).astype(jnp.float32)
    allowed = (places[None, :] <= places[:, None]) & (leading[:, None] == leading[None, :])
    return (positions, allowed)


def rotary_tables(positions):
    halves = ROT // 2
    frequency = 10000.0 ** (-(jnp.arange(halves, dtype=jnp.float32) * (2.0 / ROT)))
    angles = positions[:, None] * frequency[None, :]
    return (jnp.cos(angles), jnp.sin(angles))


def rotate(values_in, cosine_table, sine_table):
    halves = ROT // 2
    leading_half = values_in[..., :halves]
    trailing_half = values_in[..., halves:ROT]
    remainder = values_in[..., ROT:]
    cosine_rows = cosine_table[:, None, :]
    sine_rows = sine_table[:, None, :]
    return jnp.concatenate(
        [
            leading_half * cosine_rows - trailing_half * sine_rows,
            trailing_half * cosine_rows + leading_half * sine_rows,
            remainder,
        ],
        axis=-1,
    )


def masked_scores(queries, key_rows, allowed):
    scores = jnp.einsum(
        "qhd,khd->hqk", queries, key_rows, preferred_element_type=jnp.float32
    ) * HD ** (-0.5)
    return jnp.where(allowed[None], scores, -1e30)


def pick_slot(buffer, slot_at):
    return lax.dynamic_index_in_dim(buffer, slot_at, 0, keepdims=False)


def place_slot(buffer, value, slot_at, active):
    return lax.dynamic_update_index_in_dim(
        buffer, jnp.where(active, value, pick_slot(buffer, slot_at)), slot_at, 0
    )


def shards(
    inputs,
    cotangent,
    doc_split,
    qkv_weight,
    qkv_bias,
    out_weight,
    out_bias,
    fc1_weight,
    fc1_bias,
    fc2_weight,
    fc2_bias,
    ln_gain,
    ln_bias,
):
    section_at = lax.axis_index("section")
    micro_count = inputs.shape[0]
    row_count = inputs.shape[2]
    model_width = inputs.shape[3]
    slot_rows = row_count * lax.axis_size("tensor")
    local_width = qkv_bias.shape[2]
    local_heads = local_width // HD
    w_qkv, w_out, w_up, w_down = (
        lax.all_gather(qkv_weight[0], "dp", axis=0, tiled=True),
        lax.all_gather(out_weight[0], "dp", axis=1, tiled=True),
        lax.all_gather(fc1_weight[0], "dp", axis=0, tiled=True),
        lax.all_gather(fc2_weight[0], "dp", axis=1, tiled=True),
    )
    bias_qkv = qkv_bias[0]
    bias_out = out_bias[0]
    bias_up = fc1_bias[0]
    bias_down = fc2_bias[0]
    norm_gain = ln_gain[0]
    shift_term = ln_bias[0]
    splits = doc_split[:, 0]

    def layout_for(split_at):
        positions, allowed = doc_layout(split_at, slot_rows)
        cosine_table, sine_table = rotary_tables(positions)
        return (allowed, cosine_table, sine_table)

    def forward_local(normed, split_at):
        allowed, cosine_table, sine_table = layout_for(split_at)
        projected = (
            jnp.einsum("sd,dcf->scf", normed, w_qkv, preferred_element_type=jnp.float32) + bias_qkv
        )
        grouped = projected.reshape(slot_rows, 3, local_heads, HD)
        queries = rotate(grouped[:, 0], cosine_table, sine_table).astype(jnp.bfloat16)
        key_rows = rotate(grouped[:, 1], cosine_table, sine_table).astype(jnp.bfloat16)
        value_rows = grouped[:, 2].astype(jnp.bfloat16)
        scores = masked_scores(queries, key_rows, allowed)
        row_top = jnp.max(scores, axis=-1, keepdims=True)
        weights = jnp.exp(scores - row_top)
        totals = jnp.sum(weights, axis=-1, keepdims=True)
        log_total = row_top + jnp.log(totals)
        attn_probs = (weights / totals).astype(jnp.bfloat16)
        mixed_heads = jnp.einsum(
            "hqk,khd->qhd", attn_probs, value_rows, preferred_element_type=jnp.float32
        )
        mixed_heads = mixed_heads.reshape(slot_rows, local_width).astype(jnp.bfloat16)
        hidden_pre = jnp.dot(normed, w_up, preferred_element_type=jnp.float32) + bias_up
        activated = jax.nn.gelu(hidden_pre, approximate=True).astype(jnp.bfloat16)
        partial_sum = jnp.dot(mixed_heads, w_out, preferred_element_type=jnp.float32)
        partial_sum = partial_sum + jnp.dot(activated, w_down, preferred_element_type=jnp.float32)
        return (
            partial_sum,
            (queries, key_rows, value_rows, mixed_heads, log_total, hidden_pre, activated),
        )

    def spare_forward(normed, split_at):
        return jax.tree.map(jnp.zeros_like, forward_local(normed, split_at))

    def backward_local(grad_rows, kept_now, split_at):
        queries, key_rows, value_rows, mixed_heads, log_total, hidden_pre, activated = kept_now
        allowed, cosine_table, sine_table = layout_for(split_at)
        grad_mixed = jnp.einsum("sd,fd->sf", grad_rows, w_out, preferred_element_type=jnp.float32)
        grad_mixed = grad_mixed.astype(jnp.bfloat16).reshape(slot_rows, local_heads, HD)
        grad_act = jnp.einsum("sd,fd->sf", grad_rows, w_down, preferred_element_type=jnp.float32)
        gelu_back = jax.vjp(partial(jax.nn.gelu, approximate=True), hidden_pre)[1]
        grad_pre = gelu_back(grad_act)[0].astype(jnp.bfloat16)
        scores = masked_scores(queries, key_rows, allowed)
        probs = jnp.exp(scores - log_total)
        grad_values = jnp.einsum(
            "hqk,qhd->khd",
            probs.astype(jnp.bfloat16),
            grad_mixed,
            preferred_element_type=jnp.float32,
        )
        grad_probs = jnp.einsum(
            "qhd,khd->hqk", grad_mixed, value_rows, preferred_element_type=jnp.float32
        )
        centre = jnp.sum(probs * grad_probs, axis=-1, keepdims=True)
        grad_scores = (probs * (grad_probs - centre)).astype(jnp.bfloat16)
        score_scale = HD ** (-0.5)
        grad_queries = (
            jnp.einsum("hqk,khd->qhd", grad_scores, key_rows, preferred_element_type=jnp.float32)
            * score_scale
        )
        grad_keys = (
            jnp.einsum("hqk,qhd->khd", grad_scores, queries, preferred_element_type=jnp.float32)
            * score_scale
        )
        grad_queries = rotate(grad_queries, cosine_table, -sine_table)
        grad_keys = rotate(grad_keys, cosine_table, -sine_table)
        grad_proj = jnp.stack([grad_queries, grad_keys, grad_values], axis=1)
        grad_proj = grad_proj.reshape(slot_rows, 3, local_width).astype(jnp.bfloat16)
        grad_normed = jnp.einsum(
            "scf,dcf->sd", grad_proj, w_qkv, preferred_element_type=jnp.float32
        )
        grad_normed = grad_normed + jnp.einsum(
            "sf,df->sd", grad_pre, w_up, preferred_element_type=jnp.float32
        )
        return (grad_normed, (grad_proj, grad_pre))

    def spare_backward(grad_rows, kept_now, split_at):
        return jax.tree.map(jnp.zeros_like, backward_local(grad_rows, kept_now, split_at))

    def stack_zeros(example):
        return jnp.zeros((micro_count,) + example.shape, example.dtype)

    received = jnp.zeros((row_count, model_width), jnp.bfloat16)
    section_rows = jnp.zeros((micro_count, row_count, model_width), jnp.float32)
    normed_store = jnp.zeros((micro_count, slot_rows, model_width), jnp.bfloat16)
    output_store = jnp.zeros((micro_count, row_count, model_width), jnp.bfloat16)
    kept_store = None
    for moment in range(micro_count + 1):
        micro_at = moment - section_at
        active = (micro_at >= 0) & (micro_at < micro_count)
        slot_at = jnp.clip(micro_at, 0, micro_count - 1)
        own_rows = inputs[min(moment, micro_count - 1), 0].astype(jnp.float32)
        rows_now = jnp.where(section_at == 0, own_rows, received.astype(jnp.float32))
        normed_rows = layer_norm(rows_now, norm_gain, shift_term).astype(jnp.bfloat16)
        normed = lax.all_gather(normed_rows, "tensor", axis=0, tiled=True)
        split_at = pick_slot(splits, slot_at)
        partial_sum, kept_now = lax.cond(active, forward_local, spare_forward, normed, split_at)
        branch = (
            lax.psum_scatter(
                partial_sum.astype(jnp.bfloat16), "tensor", scatter_dimension=0, tiled=True
            ).astype(jnp.float32)
            + bias_out
            + bias_down
        )
        result = (rows_now + branch).astype(jnp.bfloat16)
        if kept_store is None:
            kept_store = jax.tree.map(stack_zeros, kept_now)
        kept_store = jax.tree.map(
            lambda buffer, value: place_slot(buffer, value, slot_at, active), kept_store, kept_now
        )
        section_rows = place_slot(section_rows, rows_now, slot_at, active)
        normed_store = place_slot(normed_store, normed, slot_at, active)
        output_store = place_slot(output_store, result, slot_at, active)
        received = from_behind(result, "section", 1)
    back_received = jnp.zeros((row_count, model_width), jnp.bfloat16)
    inputgrad_store = jnp.zeros((micro_count, row_count, model_width), jnp.bfloat16)
    gradrows_store = jnp.zeros((micro_count, slot_rows, model_width), jnp.bfloat16)
    proj_store = jnp.zeros((micro_count, slot_rows, 3, local_width), jnp.bfloat16)
    pre_store = jnp.zeros((micro_count, slot_rows, w_up.shape[1]), jnp.bfloat16)
    gain_total = jnp.zeros((model_width,), jnp.float32)
    shift_total = jnp.zeros((model_width,), jnp.float32)
    outbias_total = jnp.zeros((model_width,), jnp.float32)
    qkvbias_total = jnp.zeros((3, local_width), jnp.float32)
    upbias_total = jnp.zeros((w_up.shape[1],), jnp.float32)
    for moment in range(micro_count + 1):
        micro_at = moment - (1 - section_at)
        active = (micro_at >= 0) & (micro_at < micro_count)
        slot_at = jnp.clip(micro_at, 0, micro_count - 1)
        own_grad = cotangent[min(moment, micro_count - 1), 0].astype(jnp.float32)
        grad_now = jnp.where(section_at == 1, own_grad, back_received.astype(jnp.float32))
        grad_low = grad_now.astype(jnp.bfloat16)
        grad_rows = lax.all_gather(grad_low, "tensor", axis=0, tiled=True)
        kept_now = jax.tree.map(lambda buffer: pick_slot(buffer, slot_at), kept_store)
        split_at = pick_slot(splits, slot_at)
        partial_grad, grad_pieces = lax.cond(
            active, backward_local, spare_backward, grad_rows, kept_now, split_at
        )
        grad_proj, grad_pre = grad_pieces
        grad_normed = lax.psum_scatter(
            partial_grad.astype(jnp.bfloat16), "tensor", scatter_dimension=0, tiled=True
        ).astype(jnp.float32)
        rows_in = pick_slot(section_rows, slot_at)
        norm_back = jax.vjp(layer_norm, rows_in, norm_gain, shift_term)[1]
        grad_input_norm, grad_gain, grad_shift = norm_back(grad_normed)
        weight_on = active.astype(jnp.float32)
        gain_total = gain_total + weight_on * grad_gain
        shift_total = shift_total + weight_on * grad_shift
        outbias_total = outbias_total + weight_on * jnp.sum(grad_low.astype(jnp.float32), axis=0)
        qkvbias_total = qkvbias_total + jnp.sum(grad_proj.astype(jnp.float32), axis=0)
        upbias_total = upbias_total + jnp.sum(grad_pre.astype(jnp.float32), axis=0)
        grad_input = (grad_now + grad_input_norm).astype(jnp.bfloat16)
        inputgrad_store = place_slot(inputgrad_store, grad_input, slot_at, active)
        gradrows_store = place_slot(gradrows_store, grad_rows, slot_at, active)
        proj_store = place_slot(proj_store, grad_proj, slot_at, active)
        pre_store = place_slot(pre_store, grad_pre, slot_at, active)
        back_received = from_behind(grad_input, "section", -1)

    def output_terms(micro):
        rows_here = gradrows_store[micro]
        out_term = jnp.einsum(
            "sf,sd->fd", kept_store[3][micro], rows_here, preferred_element_type=jnp.float32
        )
        down_term = jnp.einsum(
            "sf,sd->fd", kept_store[6][micro], rows_here, preferred_element_type=jnp.float32
        )
        return (out_term, down_term)

    def input_terms(micro):
        normed_here = normed_store[micro]
        qkv_term = jnp.einsum(
            "sd,scf->dcf", normed_here, proj_store[micro], preferred_element_type=jnp.float32
        )
        up_term = jnp.einsum(
            "sd,sf->df", normed_here, pre_store[micro], preferred_element_type=jnp.float32
        )
        return (qkv_term, up_term)

    def summed_terms(term_fn):
        totals = term_fn(0)
        totals = tuple((held + more for held, more in zip(totals, term_fn(1))))
        return totals

    out_term, down_term = summed_terms(output_terms)
    qkv_term, up_term = summed_terms(input_terms)
    shares = (
        lax.psum_scatter(
            qkv_term.astype(jnp.bfloat16), "dp", scatter_dimension=0, tiled=True
        ).astype(jnp.float32),
        lax.psum_scatter(
            out_term.astype(jnp.bfloat16), "dp", scatter_dimension=1, tiled=True
        ).astype(jnp.float32),
        lax.psum_scatter(
            up_term.astype(jnp.bfloat16), "dp", scatter_dimension=0, tiled=True
        ).astype(jnp.float32),
        lax.psum_scatter(
            down_term.astype(jnp.bfloat16), "dp", scatter_dimension=1, tiled=True
        ).astype(jnp.float32),
    )
    qkv_bias_grad, up_bias_grad = lax.psum((qkvbias_total, upbias_total), "dp")
    gain_grad, shift_grad, outbias_grad = lax.psum(
        (gain_total, shift_total, outbias_total), ("dp", "tensor")
    )
    layer_out = output_store[None, :, None]
    input_grad = inputgrad_store[None, :, None]
    return (
        layer_out,
        input_grad,
        shares[0][None],
        qkv_bias_grad[None],
        shares[1][None],
        outbias_grad[None],
        shares[2][None],
        up_bias_grad[None],
        shares[3][None],
        outbias_grad[None],
        gain_grad[None],
        shift_grad[None],
    )


def solution(mesh):
    placed = (
        P(None, "dp", "tensor", None),
        P(None, "dp", "tensor", None),
        P(None, "dp"),
        P("section", "dp", None, "tensor"),
        P("section", None, "tensor"),
        P("section", "tensor", "dp"),
        P("section", None),
        P("section", "dp", "tensor"),
        P("section", "tensor"),
        P("section", "tensor", "dp"),
        P("section", None),
        P("section", None),
        P("section", None),
    )
    return jax.shard_map(
        shards,
        mesh=mesh,
        in_specs=placed,
        out_specs=(
            P("section", None, "dp", "tensor", None),
            P("section", None, "dp", "tensor", None),
            P("section", "dp", None, "tensor"),
            P("section", None, "tensor"),
            P("section", "tensor", "dp"),
            P("section", None),
            P("section", "dp", "tensor"),
            P("section", "tensor"),
            P("section", "tensor", "dp"),
            P("section", None),
            P("section", None),
            P("section", None),
        ),
        check_vma=False,
    )
```

profile of v0, /device:TPU:1, one launch (start us, length us, event | category | flops | bytes accessed | tf_op | source)
XLA Modules:
  0.0 1187.1 jit_solution(4399104019066142053)
XLA Ops:
  14.2 23.9 %all-gather.15.cloned.1.call-done = bf16[256,2048]{1,0:T(8,128)(2,1)} async-done(((bf16[64,2048]{1,0:T(8,128)(2,1)}), bf16[256,2048]{1,0:T(8,128)(2,1)}) %all-gather.15.cloned.1.call-update) | async-done | bytes 1048592 | tf_op jit(solution)/shard_map/all_gather | solution.py:209
  38.1 40.5 %all-gather.29.cloned.1.call-done = bf16[1,512,2048]{2,1,0:T(8,128)(2,1)} async-done(((bf16[1,512,128]{2,1,0:T(8,128)(2,1)}), bf16[1,512,2048]{2,1,0:T(8,128)(2,1)}) %all-gather.29.cloned.1.call-update) | async-done | bytes 2097168 | tf_op jit(solution)/shard_map/all_gather | solution.py:101
  78.6 44.3 %all-gather.27.cloned.1.call-done = bf16[1,2048,3,512]{3,1,2,0:T(8,128)(2,1)} async-done(((bf16[1,128,3,512]{3,1,2,0:T(8,128)(2,1)}), bf16[1,2048,3,512]{3,1,2,0:T(8,128)(2,1)}) %all-gather.27.cloned.1.call-update) | async-done | bytes 6291472 | tf_op jit(solution)/shard_map/all_gather | solution.py:100
  122.9 54.7 %all-gather.31.cloned.1.call-done = bf16[1,2048,2048]{2,1,0:T(8,128)(2,1)} async-done(((bf16[1,128,2048]{2,1,0:T(8,128)(2,1)}), bf16[1,2048,2048]{2,1,0:T(8,128)(2,1)}) %all-gather.31.cloned.1.call-update) | async-done | bytes 8388624 | tf_op jit(solution)/shard_map/all_gather | solution.py:102
  177.6 63.0 %all-gather.33.cloned.1.call-done = bf16[1,2048,2048]{2,1,0:T(8,128)(2,1)} async-done(((bf16[1,2048,128]{2,1,0:T(8,128)(2,1)}), bf16[1,2048,2048]{2,1,0:T(8,128)(2,1)}) %all-gather.33.cloned.1.call-update) | async-done | bytes 8388624 | tf_op jit(solution)/shard_map/all_gather | solution.py:103
  240.6 27.5 %conditional.6 = (bf16[256,2048]{1,0:T(8,128)(2,1)S(1)}, bf16[256,8,64]{0,2,1:T(8,128)(2,1)S(1)}, bf16[256,8,64]{0,2,1:T(8,128)(2,1)}, bf16[256,8,64]{0,2,1:T(8,...) conditional(s32[]{:T(128)} %convert_element_type.389, () %tuple.74, ...), branch_computations={%region_2.3_spmd, %region_3.6_spmd} | conditional | flops 6592072704 | bytes 151942144 | solution.py:211
  240.6 8.1 fusion.7
  270.2 20.5 %reduce-scatter.31.cloned.1.call-done = bf16[64,2048]{1,0:T(8,128)(2,1)} async-done(((bf16[256,2048]{1,0:T(8,128)(2,1)}), bf16[64,2048]{1,0:T(8,128)(2,1)}) %reduce-scatter.31.cloned.1.call-update) | async-done | bytes 262160 | tf_op jit(solution)/shard_map/reduce_scatter | solution.py:213
  301.6 26.1 %all-gather.17.cloned.1.call-done = bf16[256,2048]{1,0:T(8,128)(2,1)} async-done(((bf16[64,2048]{1,0:T(8,128)(2,1)}), bf16[256,2048]{1,0:T(8,128)(2,1)}) %all-gather.17.cloned.1.call-update) | async-done | bytes 1048592 | tf_op jit(solution)/shard_map/all_gather | solution.py:209
  327.7 31.9 %conditional.7 = (bf16[256,2048]{1,0:T(8,128)(2,1)S(1)}, bf16[256,8,64]{0,2,1:T(8,128)(2,1)S(1)}, bf16[256,8,64]{0,2,1:T(8,128)(2,1)}, bf16[256,8,64]{0,2,1:T(8,...) conditional(s32[]{:T(128)} %convert_element_type.397, () %tuple.76, ...), branch_computations={%region_9.10_spmd, %region_10.13_spmd} | conditional | flops 6592072704 | bytes 149845024 | solution.py:211
  363.3 23.0 %reduce-scatter.33.cloned.1.call-done = bf16[64,2048]{1,0:T(8,128)(2,1)} async-done(((bf16[256,2048]{1,0:T(8,128)(2,1)}), bf16[64,2048]{1,0:T(8,128)(2,1)}) %reduce-scatter.33.cloned.1.call-update) | async-done | bytes 262160 | tf_op jit(solution)/shard_map/reduce_scatter | solution.py:213
  457.8 77.6 %reduce-scatter.37.cloned.1.call-done = bf16[64,2048]{1,0:T(8,128)(2,1)} async-done(((bf16[256,2048]{1,0:T(8,128)(2,1)}), bf16[64,2048]{1,0:T(8,128)(2,1)}) %reduce-scatter.37.cloned.1.call-update) | async-done | bytes 262160 | tf_op jit(solution)/shard_map/reduce_scatter | solution.py:253
  552.9 23.3 %all-gather.23.cloned.1.call-done = bf16[256,2048]{1,0:T(8,128)(2,1)} async-done(((bf16[64,2048]{1,0:T(8,128)(2,1)}), bf16[256,2048]{1,0:T(8,128)(2,1)}) %all-gather.23.cloned.1.call-update) | async-done | bytes 1048592 | tf_op jit(solution)/shard_map/all_gather | solution.py:246
  576.2 34.7 %conditional.10 = (bf16[256,2048]{1,0:T(8,128)(2,1)S(1)}, bf16[256,3,512]{2,0,1:T(8,128)(2,1)}, bf16[256,2048]{0,1:T(8,128)(2,1)S(1)}, f32[2048]{0:T(1024)S(1)}) conditional(s32[]{:T(128)} %convert_element_type.417, () %tuple.82, (s32[2,1]{0,1:T(1,128)S(1)}, s32[]{:T(128)}, bf16[2,256,8,64]{1,3,2,0:T(8,128)(2,1)}, ...), branch_computations={%region_29.30_spmd.clone, %region_30.32_spmd.clone} | conditional | flops 6798906368 | bytes 134205960 | solution.py:249
  615.9 21.9 %reduce-scatter.39.cloned.1.call-done = bf16[64,2048]{1,0:T(8,128)(2,1)} async-done(((bf16[256,2048]{1,0:T(8,128)(2,1)}), bf16[64,2048]{1,0:T(8,128)(2,1)}) %reduce-scatter.39.cloned.1.call-update) | async-done | bytes 262160 | tf_op jit(solution)/shard_map/reduce_scatter | solution.py:253
  662.9 14.1 %all-gather.25.cloned.1.call-done = bf16[256,2048]{1,0:T(8,128)(2,1)} async-done(((bf16[64,2048]{1,0:T(8,128)(2,1)}), bf16[256,2048]{1,0:T(8,128)(2,1)}) %all-gather.25.cloned.1.call-update) | async-done | bytes 1048592 | tf_op jit(solution)/shard_map/all_gather | solution.py:246
  677.0 43.0 %conditional.11 = (bf16[256,2048]{1,0:T(8,128)(2,1)}, bf16[256,3,512]{2,0,1:T(8,128)(2,1)}, bf16[256,2048]{0,1:T(8,128)(2,1)}, f32[2048]{0:T(1024)S(1)}) conditional(s32[]{:T(128)} %convert_element_type.423, () %tuple.84, (s32[2,1]{0,1:T(1,128)S(1)}, s32[]{:T(128)}, bf16[2,256,8,64]{1,3,2,0:T(8,128)(2,1)}, ...), branch_computations={%region_37.38_spmd.clone, %region_38.40_spmd.clone} | conditional | flops 6798906368 | bytes 141545984 | solution.py:249
  772.1 8.2 fusion.134
  780.3 11.5 add_convert_fusion.12
  791.8 12.4 %copy.266 = bf16[2048,2048]{0,1:T(8,128)(2,1)} copy(bf16[2048,2048]{1,0:T(8,128)(2,1)} %add_convert_fusion.12) | data formatting | bytes 16777216
  808.1 8.2 fusion.135
  816.3 11.5 add_convert_fusion.13
  835.3 53.5 %all-reduce.1 = (f32[1,3,512]{2,0,1:T(1,128)}, f32[1,2048]{1,0:T(1,128)}) all-reduce(f32[1,3,512]{2,0,1:T(1,128)S(1)} %broadcast_in_dim.414, f32[1,2048]{1,0:T(1,128)S(1)} %bitcast.730), channel_id=1, replica_groups=mesh['section'=2,'dp'=16,'tensor'=4] {'dp'}, use_global_device_ids=true, to_apply=%region_49.50 | all-reduce | flops 3584 | bytes 28672 | tf_op jit(solution)/shard_map/psum | solution.py:313
  891.6 278.2 %all-reduce = (f32[1,2048]{1,0:T(1,128)S(1)}, f32[1,2048]{1,0:T(1,128)}, f32[1,2048]{1,0:T(1,128)}) all-reduce(f32[1,2048]{1,0:T(1,128)S(1)} %bitcast.727, f32[1,2048]{1,0:T(1,128)S(1)} %bitcast.728, f32[1,2048]{1,0:T(1,128)S(1)} %bitcast.729), channel_id=1, replica_groups=mesh['section'=2,'dp'=16,'tensor'=4] {'dp','tensor'}, use_global_device_ids=true, to_apply=%region_54.55 | all-reduce | flops 6144 | bytes 49152 | tf_op jit(solution)/shard_map/psum | solution.py:314
  (535 shorter events, 353.7 us)
Async XLA Ops:
  7.2 30.9 %all-gather.15.cloned.1.call-start = ((), (), s32[]{:S(2)}) async-start(), calls=%async_computation.10 | async-start | bytes 1310720 | tf_op jit(solution)/shard_map/all_gather | solution.py:209
  11.5 67.1 %all-gather.29.cloned.1.call-start = ((), (), s32[]{:S(2)}) async-start(), calls=%async_computation.19 | async-start | bytes 2228224 | tf_op jit(solution)/shard_map/all_gather | solution.py:101
  12.2 110.7 %all-gather.27.cloned.1.call-start = ((), (), s32[]{:S(2)}) async-start(), calls=%async_computation.18 | async-start | bytes 6684672 | tf_op jit(solution)/shard_map/all_gather | solution.py:100
  12.9 164.6 %all-gather.31.cloned.1.call-start = ((), (), s32[]{:S(2)}) async-start(), calls=%async_computation.20 | async-start | bytes 8912896 | tf_op jit(solution)/shard_map/all_gather | solution.py:102
  13.5 227.0 %all-gather.33.cloned.1.call-start = ((), (), s32[]{:S(2)}) async-start(), calls=%async_computation.21 | async-start | bytes 8912896 | tf_op jit(solution)/shard_map/all_gather | solution.py:103
  14.1 276.6 %reduce-scatter.31.cloned.1.call-start = ((), (), s32[]{:S(2)}) async-start(), calls=%async_computation.22 | async-start | bytes 1310720 | tf_op jit(solution)/shard_map/reduce_scatter | solution.py:213
  270.1 57.6 %all-gather.17.cloned.1.call-start = ((), (), s32[]{:S(2)}) async-start(), calls=%async_computation.11 | async-start | bytes 1310720 | tf_op jit(solution)/shard_map/all_gather | solution.py:209
  291.9 8.1 collective-permute-start
  301.3 85.0 %reduce-scatter.33.cloned.1.call-start = ((), (), s32[]{:S(2)}) async-start(), calls=%async_computation.23 | async-start | bytes 1310720 | tf_op jit(solution)/shard_map/reduce_scatter | solution.py:213
  363.2 72.5 %all-gather.19.cloned.1.call-start = ((), (), s32[]{:S(2)}) async-start(), calls=%async_computation.12 | async-start | bytes 1310720 | tf_op jit(solution)/shard_map/all_gather | solution.py:209
  387.5 8.0 collective-permute-start.1
  396.9 54.2 %all-gather.21.cloned.1.call-start = ((), (), s32[]{:S(2)}) async-start(), calls=%async_computation.13 | async-start | bytes 1310720 | tf_op jit(solution)/shard_map/all_gather | solution.py:246
  398.3 137.1 %reduce-scatter.37.cloned.1.call-start = ((), (), s32[]{:S(2)}) async-start(), calls=%async_computation.25 | async-start | bytes 1310720 | tf_op jit(solution)/shard_map/reduce_scatter | solution.py:253
  456.9 119.3 %all-gather.23.cloned.1.call-start = ((), (), s32[]{:S(2)}) async-start(), calls=%async_computation.14 | async-start | bytes 1310720 | tf_op jit(solution)/shard_map/all_gather | solution.py:246
  540.8 9.2 collective-permute-start.2
  552.5 85.3 %reduce-scatter.39.cloned.1.call-start = ((), (), s32[]{:S(2)}) async-start(), calls=%async_computation.26 | async-start | bytes 1310720 | tf_op jit(solution)/shard_map/reduce_scatter | solution.py:253
  614.7 62.3 %all-gather.25.cloned.1.call-start = ((), (), s32[]{:S(2)}) async-start(), calls=%async_computation.15 | async-start | bytes 1310720 | tf_op jit(solution)/shard_map/all_gather | solution.py:246
  642.5 8.6 collective-permute-start.3
  651.9 177.8 %reduce-scatter.35.cloned.1.call-start = ((), (), s32[]{:S(2)}) async-start(), calls=%async_computation.24 | async-start | bytes 1310720 | tf_op jit(solution)/shard_map/reduce_scatter | solution.py:213
  654.9 233.8 %reduce-scatter.41.cloned.1.call-start = ((), (), s32[]{:S(2)}) async-start(), calls=%async_computation.27 | async-start | bytes 1310720 | tf_op jit(solution)/shard_map/reduce_scatter | solution.py:253
  724.6 446.5 %reduce-scatter.43.cloned.1.call-start = ((), (), s32[]{:S(2)}) async-start(), calls=%async_computation.28 | async-start | bytes 2228224
  742.9 430.2 %reduce-scatter.27.cloned.1.call-start = ((), (), s32[]{:S(2)}) async-start(), calls=%async_computation.16 | async-start | bytes 6684672 | tf_op jit(solution)/shard_map/reduce_scatter | solution.py:300
  768.4 406.6 %reduce-scatter.45.cloned.1.call-start = ((), (), s32[]{:S(2)}) async-start(), calls=%async_computation.29 | async-start | bytes 8912896
  804.2 373.1 %reduce-scatter.29.cloned.1.call-start = ((), (), s32[]{:S(2)}) async-start(), calls=%async_computation.17 | async-start | bytes 8912896 | tf_op jit(solution)/shard_map/reduce_scatter | solution.py:306
  (99 other events, 1907.0 us)
Sparse Core Ops, SparseCore 0:
  11.6 26.4 all-gather.14
  39.7 38.8 all-gather.28
  80.3 42.5 all-gather.26
  124.5 53.0 all-gather.30
  179.0 61.4 all-gather.32
  270.2 20.4 reduce-scatter.30
  301.5 26.1 all-gather.16
  363.3 22.9 reduce-scatter.32
  397.0 27.0 all-gather.18
  425.6 24.5 all-gather.20
  457.0 78.3 reduce-scatter.36
  552.6 23.5 all-gather.22
  614.8 22.9 reduce-scatter.38
  652.1 24.8 all-gather.24
  679.2 23.2 reduce-scatter.34
  724.7 21.4 reduce-scatter.40
  748.5 62.5 reduce-scatter.42
  813.3 78.7 reduce-scatter.26
  894.5 98.1 reduce-scatter.44
  994.9 97.2 reduce-scatter.28
where the time goes:
time: 1200 us; the launch traced here: 1190 us
  waiting for transfers between devices  458 us (38%)
  blocking collectives  332 us (28%)
  local copies, waits for them, and re-layouts  151 us (13%)
  matrix products  128 us (11%)
  other arithmetic  87.5 us (7%)
  between operations  15.6 us (1%)
  starting transfers between devices  14.4 us (1%)
    psum x1, blocking collectives, shards(): lax.psum((gain_total, shift_total, outbias_total), ('dp', 'tensor'))  278 us
    reduce_scatter x3, waiting for transfers between devices, shards(): lax.psum_scatter(partial_grad.astype(jnp.bfloat16), 'tensor', scatter_dim...  99.5 us
    all_gather x1, waiting for transfers between devices, shards(): lax.all_gather(fc2_weight[0], 'dp', axis=1, tiled=True)  63 us
    all_gather x1, waiting for transfers between devices, shards(): lax.all_gather(fc1_weight[0], 'dp', axis=0, tiled=True)  54.7 us
    psum x1, blocking collectives, shards(): qkv_bias_grad, up_bias_grad = lax.psum((qkvbias_total, upbias_total), 'dp')  53.5 us
    all_gather x3, waiting for transfers between devices, shards(): normed = lax.all_gather(normed_rows, 'tensor', axis=0, tiled=True)  50.1 us
    unnamed x121, local copies, waits for them, and re-layouts  44.7 us
    all_gather x1, waiting for transfers between devices, shards(): lax.all_gather(qkv_weight[0], 'dp', axis=0, tiled=True)  44.3 us
  transfers between devices with their start and end apart: 24, of which 16 were waited for; matrix products, arithmetic and copies ran while one was open for 18% of the time, Pallas kernels for 0%

commit v1 on v0

v1 whole, which is shorter than its diff:
```python
from functools import partial

import jax
import jax.numpy as jnp
import numpy as np
from jax import lax
from jax.experimental import pallas as pl
from jax.experimental.pallas import tpu as pltpu
from jax.sharding import PartitionSpec as P

HD = 64
ROT = 32
EPSILON = 1e-05
MESH = pl.DeviceIdType.MESH
BF = jnp.bfloat16
F32 = jnp.float32

D = 2048
SLOT = 256
ROWS = 64
QKV = 768
UP = 1024
A_COLS = QKV + UP
MIX = 256
B_COLS = MIX + UP
COLS = A_COLS + B_COLS
A_HALF = A_COLS // 2
B_HALF = B_COLS // 2
MIB = 2**20


def dot(a, b):
    return lax.dot_general(a, b, (((1,), (0,)), ((), ())), preferred_element_type=F32)


def dot_nt(a, b):
    return lax.dot_general(a, b, (((1,), (1,)), ((), ())), preferred_element_type=F32)


def dot_tn(a, b):
    return lax.dot_general(a, b, (((0,), (0,)), ((), ())), preferred_element_type=F32)


def remote(src, dst, send, recv, device):
    return pltpu.make_async_remote_copy(
        src_ref=src, dst_ref=dst, send_sem=send, recv_sem=recv, device_id=device, device_id_type=MESH
    )


def greet(peers):
    barrier = pltpu.get_barrier_semaphore()
    for peer in peers:
        pl.semaphore_signal(barrier, inc=1, device_id=peer, device_id_type=MESH)
    pl.semaphore_wait(barrier, len(peers))


class Place:
    def __init__(self):
        self.dp = lax.axis_index("dp")
        self.core = lax.rem(self.dp, 2)
        self.x = lax.rem(self.dp // 2, 2)
        self.y = self.dp // 4
        self.z = lax.axis_index("tensor")
        self.sibling = {"dp": self.dp + 1 - 2 * self.core}
        self.across = {"dp": self.at(self.y, 1 - self.x, self.core)}

    def at(self, y, x, core):
        return (y * 2 + x) * 2 + core

    def turn(self, by):
        return lax.rem(self.y + 4 + by, 4)

    def beside(self, by):
        return {"dp": self.at(self.turn(by), self.x, self.core)}

    def z_peer(self, by):
        return {"tensor": lax.rem(self.z + by, 4)}


def gather_kernel(block, split, w, their_split, own_sem, x_send, x_recv, y_send, y_recv, sib_send, sib_recv):
    me = Place()
    greet([me.sibling, me.across, me.beside(1), me.beside(-1)])

    def rows(dp):
        return pl.ds(pl.multiple_of(dp * 128, 128), 128)

    def chip(y, x):
        return pl.ds(pl.multiple_of((y * 2 + x) * 256, 256), 256)

    other = me.dp + 1 - 2 * me.core
    keep = pltpu.make_async_copy(block.at[me.core], w.at[rows(me.dp)], own_sem)
    keep.start()
    give = remote(block.at[1 - me.core], w.at[rows(me.dp)], sib_send.at[0], sib_recv.at[0], me.sibling)
    give.start()
    tell = remote(split, their_split, sib_send.at[1], sib_recv.at[1], me.sibling)
    tell.start()
    keep.wait()
    remote(block.at[1 - me.core], w.at[rows(other)], sib_send.at[0], sib_recv.at[0], me.sibling).wait_recv()

    cols = [
        pl.ds(0, A_HALF),
        pl.ds(A_HALF, A_HALF),
        pl.ds(A_COLS, B_HALF),
        pl.ds(A_COLS + B_HALF, B_HALF),
    ]

    def part(y, x, which):
        return w.at[chip(y, x), cols[which]]

    def over_x(y, x, which, slot):
        piece = part(y, x, which)
        return remote(piece, piece, x_send.at[slot], x_recv.at[slot], me.across)

    def over_y(by, y, x, which, slot):
        piece = part(y, x, which)
        way = 0 if by > 0 else 1
        return remote(piece, piece, y_send.at[way, slot], y_recv.at[way, slot], me.beside(by))

    sent = []

    def start(copy):
        copy.start()
        sent.append(copy)

    y, x = me.y, me.x
    for which in (0, 1):
        start(over_x(y, x, which, which))
    for which in (2, 3):
        for by in (1, -1):
            start(over_y(by, y, x, which, which))
    for which in (2, 3):
        start(over_x(y, x, which, which))
    for which in (0, 1):
        for by in (1, -1):
            start(over_y(by, y, x, which, which))
    for which in (2, 3):
        for by in (1, -1):
            source = me.turn(-by)
            over_y(by, source, x, which, which).wait_recv()
            if (which == 2) == (by > 0):
                start(over_y(by, source, x, which, 6))
            start(over_x(source, x, which, 2 * which + (0 if by > 0 else 1)))
    for which in (0, 1):
        over_x(y, 1 - x, which, which).wait_recv()
        for by in (1, -1):
            start(over_y(by, y, 1 - x, which, 4 + which))
    far = me.turn(2)
    for which, by in ((2, 1), (3, -1)):
        over_y(by, far, x, which, 6).wait_recv()
        start(over_x(far, x, which, 6 + which))
    for which, by in ((0, 1), (1, -1)):
        source = me.turn(-by)
        over_y(by, source, x, which, which).wait_recv()
        start(over_y(by, source, x, which, 7))
    for which, by in ((0, 1), (1, -1)):
        source = me.turn(-by)
        over_y(by, source, 1 - x, which, 4 + which).wait_recv()
        start(over_y(by, source, 1 - x, which, 8))
    for which, by in ((0, -1), (1, 1)):
        source = me.turn(-by)
        over_y(by, source, x, which, which).wait_recv()
        over_y(by, source, 1 - x, which, 4 + which).wait_recv()
    for which in (2, 3):
        over_x(y, 1 - x, which, which).wait_recv()
        for by in (1, -1):
            over_x(me.turn(-by), 1 - x, which, 2 * which + (0 if by > 0 else 1)).wait_recv()
        over_x(far, 1 - x, which, 6 + which).wait_recv()
    for which, by in ((0, 1), (1, -1)):
        over_y(by, far, x, which, 7).wait_recv()
        over_y(by, far, 1 - x, which, 8).wait_recv()
    for copy in sent:
        copy.wait_send()
    give.wait_send()
    tell.wait()


def gather_weights(block, split):
    return pl.pallas_call(
        gather_kernel,
        out_shape=(jax.ShapeDtypeStruct((D, COLS), BF), jax.ShapeDtypeStruct(split.shape, split.dtype)),
        in_specs=[pl.BlockSpec(memory_space=pl.ANY)] * 2,
        out_specs=[pl.BlockSpec(memory_space=pl.ANY)] * 2,
        scratch_shapes=[
            pltpu.SemaphoreType.DMA,
            pltpu.SemaphoreType.DMA((10,)),
            pltpu.SemaphoreType.DMA((10,)),
            pltpu.SemaphoreType.DMA((2, 9)),
            pltpu.SemaphoreType.DMA((2, 9)),
            pltpu.SemaphoreType.DMA((2,)),
            pltpu.SemaphoreType.DMA((2,)),
        ],
        compiler_params=pltpu.CompilerParams(collective_id=1, has_side_effects=True),
        name="gather_weights",
    )(block, split)


def middle_kernel(
    x_ref, cot_ref, w_hbm, ba_ref, bb_ref, gain_ref, shift_ref, mine_ref, theirs_ref, cos_ref, sin_ref,
    lo_ref, ig_ref, n_out, h_out, g_out, p_out, sa_ref, sb_ref,
    w, normed, grads, qkv, hcat, slope, probs, gproj, part, got, zgot, xrow, grow, ctab, stab, split,
    wsem, agz_s, agz_r, ags_s, ags_r, par_s, par_r, rsz_s, rsz_r, sec_s, sec_r, osem,
):
    me = Place()
    section = lax.axis_index("section")
    core, z = me.core, me.z
    greet([me.z_peer(1), me.z_peer(2), me.z_peer(3), me.sibling, {"section": 1 - section}])

    load_a = pltpu.make_async_copy(w_hbm.at[:, pl.ds(0, A_COLS)], w.at[:, pl.ds(0, A_COLS)], wsem.at[0])
    load_b = pltpu.make_async_copy(w_hbm.at[:, pl.ds(A_COLS, B_COLS)], w.at[:, pl.ds(A_COLS, B_COLS)], wsem.at[1])

    def band(at):
        return pl.ds(pl.multiple_of(at * ROWS, ROWS), ROWS)

    def standard(rows):
        average = jnp.mean(rows, axis=-1, keepdims=True)
        centred = rows - average
        variance = jnp.mean(centred * centred, axis=-1, keepdims=True)
        scale = lax.rsqrt(variance + EPSILON)
        return centred * scale, scale

    def spread_buffer(back):
        return grads if back else normed

    def to_z(back, m, i, k):
        piece = spread_buffer(back).at[i, band(z)]
        return remote(piece, piece, agz_s.at[back, m, k], agz_r.at[back, m, k], me.z_peer(1 + k))

    def from_z(back, m, i, k):
        piece = spread_buffer(back).at[i, band(lax.rem(z + 3 - k, 4))]
        return remote(piece, piece, agz_s.at[back, m, k], agz_r.at[back, m, k], me.z_peer(3 - k))

    def to_sibling(back, m, i, k):
        piece = spread_buffer(back).at[i, band(lax.rem(z + 3 - k, 4))]
        return remote(piece, piece, ags_s.at[back, m, k], ags_r.at[back, m, k], me.sibling)

    def spread_own(back, m):
        i = 2 * m + core
        if back:
            grads[i, band(z)] = grow[m]
        else:
            xhat, _ = standard(xrow[m].astype(F32))
            normed[i, band(z)] = (xhat * gain_ref[...] + shift_ref[...]).astype(BF)
        for k in range(3):
            to_z(back, m, i, k).start()
        to_sibling(back, m, i, 3).start()

    def relay(back, i):
        m = i // 2
        for k in range(3):
            from_z(back, m, i, k).wait_recv()
            to_sibling(back, m, i, k).start()

    def await_rows(back, i):
        m = i // 2

        @pl.when(lax.rem(i, 2) != core)
        def _():
            for k in range(4):
                to_sibling(back, m, i, k).wait_recv()

    def to_pair(back, i):
        m = i // 2
        return remote(part.at[back * 4 + i], got.at[back * 2 + m], par_s.at[back, m], par_r.at[back, m], me.sibling)

    def sum_to_z(back, m, i, k):
        peer = me.z_peer(1 + k)
        return remote(
            part.at[back * 4 + i, band(peer["tensor"])],
            zgot.at[back * 2 + m, k],
            rsz_s.at[back, m, k],
            rsz_r.at[back, m, k],
            peer,
        )

    def pair_sum(back, i):
        m = i // 2
        to_pair(back, i).wait_recv()
        at = back * 4 + i
        part[at] = (part[at].astype(F32) + got[back * 2 + m].astype(F32)).astype(BF)
        for k in range(3):
            sum_to_z(back, m, i, k).start()

    def row_sum(back, i):
        m = i // 2
        total = part[back * 4 + i, band(z)].astype(F32)
        for k in range(3):
            sum_to_z(back, m, i, k).wait_recv()
            total = total + zgot[back * 2 + m, k].astype(F32)
        return total

    def onward(back, m):
        source, target = (ig_ref, grow) if back else (lo_ref, xrow)
        return remote(source.at[m], target.at[m], sec_s.at[back, m], sec_r.at[back, m], {"section": 1 - back})

    def finish_forward(i):
        m = i // 2
        lo_ref[m] = (xrow[m].astype(F32) + row_sum(0, i) + bb_ref[...]).astype(BF)

        @pl.when(section == 0)
        def _():
            onward(0, m).start()

    def finish_backward(i):
        m = i // 2
        grad = row_sum(1, i)
        xhat, scale = standard(xrow[m].astype(F32))
        above = grow[m].astype(F32)
        sb_ref[0:1, :] += jnp.sum(grad * xhat, axis=0, keepdims=True)
        sb_ref[1:2, :] += jnp.sum(grad, axis=0, keepdims=True)
        sb_ref[2:3, :] += jnp.sum(above, axis=0, keepdims=True)
        a = grad * gain_ref[...]
        inner = a - jnp.mean(a, axis=-1, keepdims=True) - xhat * jnp.mean(a * xhat, axis=-1, keepdims=True)
        ig_ref[m] = (above + inner * scale).astype(BF)

        @pl.when(section == 1)
        def _():
            onward(1, m).start()

    lanes = lax.broadcasted_iota(jnp.int32, (SLOT, 128), 1) % HD
    early = lanes < ROT // 2

    def turned(values, i, sign):
        halves = []
        for at in (0, 128):
            piece = values[:, at : at + 128]
            swapped = jnp.where(early, pltpu.roll(piece, 128 - ROT // 2, 1), pltpu.roll(piece, ROT // 2, 1))
            halves.append(piece * ctab[i] + swapped * (stab[i] * sign))
        return jnp.concatenate(halves, axis=1)

    def head_mask(head):
        lane = lax.broadcasted_iota(jnp.int32, (1, MIX), 1)
        return jnp.where(lane // HD == head, 1.0, 0.0).astype(BF)

    def forward_first(i):
        rows = normed[i]
        projected = dot(rows, w[:, 0:QKV]) + ba_ref[0:1, 0:QKV]
        queries = turned(projected[:, 0:MIX], i, 1.0).astype(BF)
        keys = turned(projected[:, MIX : 2 * MIX], i, 1.0).astype(BF)
        values = projected[:, 2 * MIX : 3 * MIX].astype(BF)
        qkv[i, :, 0:MIX] = queries
        qkv[i, :, MIX : 2 * MIX] = keys
        qkv[i, :, 2 * MIX : 3 * MIX] = values
        at = split[pl.ds(i, 1), :]
        at = jnp.concatenate([at, at], axis=1)
        row_at = lax.broadcasted_iota(jnp.int32, (SLOT, SLOT), 0)
        key_at = lax.broadcasted_iota(jnp.int32, (SLOT, SLOT), 1)
        same = jnp.where(row_at < at, 1, 0) == jnp.where(key_at < at, 1, 0)
        allowed = (key_at <= row_at) & same
        mixed = jnp.zeros((SLOT, MIX), F32)
        for head in range(4):
            mask = head_mask(head)
            scores = jnp.where(allowed, dot_nt(queries * mask, keys) * HD**-0.5, -1e30)
            weights = jnp.exp(scores - jnp.max(scores, axis=-1, keepdims=True))
            chances = (weights / jnp.sum(weights, axis=-1, keepdims=True)).astype(BF)
            probs[i, head] = chances
            mixed = mixed + dot(chances, values * mask)
        hcat[i, :, 0:MIX] = mixed.astype(BF)
        v = dot(rows, w[:, QKV:A_COLS]) + ba_ref[0:1, QKV:A_COLS]
        root = np.sqrt(2 / np.pi).astype(np.float32)
        square = v * v
        bent = jnp.tanh(root * (v + 0.044715 * (square * v)))
        half = 0.5 * (1.0 + bent)
        hcat[i, :, MIX:B_COLS] = (v * half).astype(BF)
        slope[i] = (half + 0.5 * v * (1.0 - bent * bent) * (root * (1.0 + 3 * 0.044715 * square))).astype(BF)

    def forward_second(i):
        part[i] = dot_nt(hcat[i], w[:, A_COLS:COLS]).astype(BF)

    def backward_first(i):
        grad_hidden = dot(grads[i], w[:, A_COLS:COLS])
        grad_pre = (grad_hidden[:, MIX:B_COLS] * slope[i].astype(F32)).astype(BF)
        gproj[i, :, QKV:A_COLS] = grad_pre
        sa_ref[0:1, QKV:A_COLS] += jnp.sum(grad_pre.astype(F32), axis=0, keepdims=True)
        grad_mixed = grad_hidden[:, 0:MIX].astype(BF)
        queries = qkv[i, :, 0:MIX]
        keys = qkv[i, :, MIX : 2 * MIX]
        values = qkv[i, :, 2 * MIX : 3 * MIX]
        zero = jnp.zeros((SLOT, MIX), F32)
        grad_queries, grad_keys, grad_values = zero, zero, zero
        for head in range(4):
            mask = head_mask(head)
            chances = probs[i, head]
            masked = grad_mixed * mask
            grad_values = grad_values + dot_tn(chances, masked)
            grad_probs = dot_nt(masked, values)
            wide = chances.astype(F32)
            centre = jnp.sum(wide * grad_probs, axis=-1, keepdims=True)
            grad_scores = (wide * (grad_probs - centre)).astype(BF)
            grad_queries = grad_queries + dot(grad_scores, keys * mask)
            grad_keys = grad_keys + dot_tn(grad_scores, queries * mask)
        pieces = (
            turned(grad_queries * HD**-0.5, i, -1.0).astype(BF),
            turned(grad_keys * HD**-0.5, i, -1.0).astype(BF),
            grad_values.astype(BF),
        )
        for at, piece in enumerate(pieces):
            span = slice(at * MIX, (at + 1) * MIX)
            gproj[i, :, span] = piece
            sa_ref[0:1, span] += jnp.sum(piece.astype(F32), axis=0, keepdims=True)

    def backward_second(i):
        part[4 + i] = dot_nt(gproj[i], w[:, 0:A_COLS]).astype(BF)

    def keep(which, i):
        source, target = ((normed, n_out), (hcat, h_out), (grads, g_out), (gproj, p_out))[which]
        return pltpu.make_async_copy(source.at[i], target.at[i], osem.at[which, i])

    load_a.start()
    load_b.start()
    sa_ref[...] = jnp.zeros_like(sa_ref)
    sb_ref[...] = jnp.zeros_like(sb_ref)

    @pl.when(section == 0)
    def _():
        xrow[...] = x_ref[...]
        for m in range(2):
            spread_own(0, m)

    @pl.when(section == 1)
    def _():
        grow[...] = cot_ref[...]
        for m in range(2):
            spread_own(1, m)

    places = lax.broadcasted_iota(jnp.int32, (SLOT, 128), 0)
    sign = jnp.where(early, -1.0, 1.0)
    for i in range(4):
        at = jnp.where(core == i % 2, mine_ref[i // 2 : i // 2 + 1, :], theirs_ref[i // 2 : i // 2 + 1, :])
        split[i : i + 1, :] = at
        first = places < at
        here = places == at
        cosine, sine = cos_ref[...], sin_ref[...]
        cos_at = jnp.sum(jnp.where(here, cosine, 0.0), axis=0, keepdims=True)
        sin_at = jnp.sum(jnp.where(here, sine, 0.0), axis=0, keepdims=True)
        ctab[i] = jnp.where(first, cosine, cosine * cos_at + sine * sin_at)
        stab[i] = jnp.where(first, sine, sine * cos_at - cosine * sin_at) * sign

    @pl.when((section == 1) & (core == 0))
    def _():
        onward(0, 0).wait_recv()
        spread_own(0, 0)

    @pl.when(core == 0)
    def _():
        relay(0, 0)

    load_a.wait()
    load_b.wait()

    def forward_step(i, _):
        own = lax.rem(i, 2) == core

        @pl.when((section == 1) & (i < 3) & jnp.logical_not(own))
        def _():
            onward(0, (i + 1) // 2).wait_recv()
            spread_own(0, (i + 1) // 2)

        @pl.when(i < 4)
        def _():
            await_rows(0, i)
            forward_first(i)

        @pl.when((i < 3) & jnp.logical_not(own))
        def _():
            relay(0, i + 1)

        @pl.when((i >= 1) & (i < 5) & jnp.logical_not(own))
        def _():
            pair_sum(0, i - 1)

        @pl.when((i >= 2) & own)
        def _():
            finish_forward(i - 2)

        @pl.when(i < 4)
        def _():
            forward_second(i)
            keep(0, i).start()
            keep(1, i).start()

            @pl.when(jnp.logical_not(own))
            def _():
                to_pair(0, i).start()

        return 0

    lax.fori_loop(0, 6, forward_step, 0)

    @pl.when((section == 0) & (core == 0))
    def _():
        onward(1, 0).wait_recv()
        spread_own(1, 0)

    @pl.when(core == 0)
    def _():
        relay(1, 0)

    def backward_step(i, _):
        own = lax.rem(i, 2) == core

        @pl.when((section == 0) & (i < 3) & jnp.logical_not(own))
        def _():
            onward(1, (i + 1) // 2).wait_recv()
            spread_own(1, (i + 1) // 2)

        @pl.when(i < 4)
        def _():
            await_rows(1, i)
            backward_first(i)

        @pl.when((i < 3) & jnp.logical_not(own))
        def _():
            relay(1, i + 1)

        @pl.when((i >= 1) & (i < 5) & jnp.logical_not(own))
        def _():
            pair_sum(1, i - 1)

        @pl.when((i >= 2) & own)
        def _():
            finish_backward(i - 2)

        @pl.when(i < 4)
        def _():
            backward_second(i)
            keep(2, i).start()
            keep(3, i).start()

            @pl.when(jnp.logical_not(own))
            def _():
                to_pair(1, i).start()

        return 0

    lax.fori_loop(0, 6, backward_step, 0)

    for back in range(2):
        for m in range(2):
            mine = 2 * m + core
            for k in range(3):
                to_z(back, m, mine, k).wait_send()
                sum_to_z(back, m, mine, k).wait_send()
            for k in range(4):
                to_sibling(back, m, mine, k).wait_send()
            to_pair(back, 2 * m + 1 - core).wait_send()

        @pl.when(section == back)
        def _():
            for m in range(2):
                onward(back, m).wait_send()

    for which in range(4):
        for i in range(4):
            keep(which, i).wait()


def middle(rows_in, cotangent, w, bias_a, bias_b, gain, shift, mine, theirs):
    places = np.arange(SLOT, dtype=np.float32)
    frequency = (10000.0 ** (-(np.arange(ROT // 2, dtype=np.float32) * np.float32(2.0 / ROT)))).astype(np.float32)
    angles = (places[:, None] * frequency[None, :]).astype(np.float32).astype(np.float64)
    cosine = np.ones((SLOT, HD), np.float32)
    sine = np.zeros((SLOT, HD), np.float32)
    cosine[:, 0:ROT] = np.tile(np.cos(angles), (1, 2))
    sine[:, 0:ROT] = np.tile(np.sin(angles), (1, 2))
    cosine, sine = (jnp.asarray(np.tile(table, (1, 2))) for table in (cosine, sine))
    any_ = pl.BlockSpec(memory_space=pl.ANY)
    vmem = pl.BlockSpec(memory_space=pltpu.VMEM)
    dma = pltpu.SemaphoreType.DMA
    return pl.pallas_call(
        middle_kernel,
        out_shape=(
            jax.ShapeDtypeStruct((2, ROWS, D), BF),
            jax.ShapeDtypeStruct((2, ROWS, D), BF),
            jax.ShapeDtypeStruct((4, SLOT, D), BF),
            jax.ShapeDtypeStruct((4, SLOT, B_COLS), BF),
            jax.ShapeDtypeStruct((4, SLOT, D), BF),
            jax.ShapeDtypeStruct((4, SLOT, A_COLS), BF),
            jax.ShapeDtypeStruct((8, A_COLS), F32),
            jax.ShapeDtypeStruct((8, D), F32),
        ),
        in_specs=[vmem, vmem, any_] + [vmem] * 8,
        out_specs=[vmem, vmem] + [any_] * 4 + [vmem, vmem],
        scratch_shapes=[
            pltpu.VMEM((D, COLS), BF),
            pltpu.VMEM((4, SLOT, D), BF),
            pltpu.VMEM((4, SLOT, D), BF),
            pltpu.VMEM((4, SLOT, QKV), BF),
            pltpu.VMEM((4, SLOT, B_COLS), BF),
            pltpu.VMEM((4, SLOT, UP), BF),
            pltpu.VMEM((4, 4, SLOT, SLOT), BF),
            pltpu.VMEM((4, SLOT, A_COLS), BF),
            pltpu.VMEM((8, SLOT, D), BF),
            pltpu.VMEM((4, SLOT, D), BF),
            pltpu.VMEM((4, 3, ROWS, D), BF),
            pltpu.VMEM((2, ROWS, D), BF),
            pltpu.VMEM((2, ROWS, D), BF),
            pltpu.VMEM((4, SLOT, 128), F32),
            pltpu.VMEM((4, SLOT, 128), F32),
            pltpu.VMEM((8, 128), jnp.int32),
            dma((2,)),
            dma((2, 2, 3)),
            dma((2, 2, 3)),
            dma((2, 2, 4)),
            dma((2, 2, 4)),
            dma((2, 2)),
            dma((2, 2)),
            dma((2, 2, 3)),
            dma((2, 2, 3)),
            dma((2, 2)),
            dma((2, 2)),
            dma((4, 4)),
        ],
        compiler_params=pltpu.CompilerParams(
            collective_id=2, has_side_effects=True, vmem_limit_bytes=62 * MIB
        ),
        name="both_layers",
    )(rows_in, cotangent, w, bias_a, bias_b, gain, shift, mine, theirs, cosine, sine)


def weights_kernel(
    n_hbm, p_hbm, g_hbm, h_hbm, sa_ref, sb_ref, out, sums_ref,
    rows_n, rows_p, rows_g, rows_h, xb_out, xb_in, far_a, far_b, half_a, half_b, near_a, near_b, got_a, got_b,
    xa_out, xa_in, done, tally, came, lsem, xs, xr, fs, fr, ns, nr, ss, sr, osem, ts, tr,
):
    me = Place()
    x, y, core = me.x, me.y, me.core
    loads = [
        pltpu.make_async_copy(source, target, lsem.at[at])
        for at, (source, target) in enumerate(
            ((g_hbm, rows_g), (h_hbm, rows_h), (n_hbm, rows_n), (p_hbm, rows_p))
        )
    ]
    for load in loads:
        load.start()
    near_z = {"tensor": me.z + 1 - 2 * lax.rem(me.z, 2)}
    near_y = {"dp": me.at(y + 1 - 2 * lax.rem(y, 2), x, core)}
    greet([me.sibling, me.across, me.beside(1), me.beside(-1), me.beside(2), me.z_peer(1), me.z_peer(2), me.z_peer(3)])
    sent = []

    partners = (me.across, near_y, me.beside(2), near_z, me.z_peer(2), me.sibling)

    def exchange(step):
        return remote(tally.at[step], came.at[step], ts.at[step], tr.at[step], partners[step])

    def fold(step):
        exchange(step).wait_recv()
        total = tally[step] + came[step]
        if step < 3:
            tally[step + 1] = total
        else:
            tally[step + 1, 0:3] = total[0:3]
            tally[step + 1, 3:8] = tally[step, 3:8]
        if step < 5:
            start(exchange(step + 1))

    def start(copy):
        copy.start()
        sent.append(copy)

    tally[0, 0:3] = sb_ref[0:3]
    tally[0, 3:8] = jnp.zeros((5, D), F32)
    tally[0, 3:4, 0:A_COLS] = sa_ref[0:1]
    start(exchange(0))

    def chip(by, x_at):
        return pl.ds(pl.multiple_of((me.turn(by) * 2 + x_at) * 256, 256), 256)

    def term_a(by, x_at):
        return dot_tn(rows_n[:, chip(by, x_at)], rows_p[...])

    def term_b(by, x_at):
        return dot_tn(rows_g[:, chip(by, x_at)], rows_h[...])

    first_a, second_a = pl.ds(0, A_HALF), pl.ds(A_HALF, A_HALF)
    first_b, second_b = pl.ds(0, B_HALF), pl.ds(B_HALF, B_HALF)

    def cross(k):
        return remote(xb_out.at[k], xb_in.at[k], xs.at[k], xr.at[k], me.across)

    def cross_last():
        return remote(xa_out, xa_in, xs.at[4], xr.at[4], me.across)

    def far_piece(way, x_at):
        by = 1 - 2 * way
        return remote(
            far_a.at[x_at, :, (first_a, second_a)[way]], half_a.at[way, x_at], fs.at[way, x_at], fr.at[way, x_at], me.beside(by)
        )

    def far_piece_b(way):
        by = 1 - 2 * way
        return remote(far_b.at[:, (first_b, second_b)[way]], half_b.at[way], fs.at[way, 2], fr.at[way, 2], me.beside(by))

    def near_piece(way, x_at):
        by = 1 - 2 * way
        return remote(near_a.at[way, x_at], got_a.at[way, x_at], ns.at[way, x_at], nr.at[way, x_at], me.beside(by))

    def near_piece_b(way):
        by = 1 - 2 * way
        return remote(near_b.at[way], got_b.at[way], ns.at[way, 2], nr.at[way, 2], me.beside(by))

    loads[0].wait()
    loads[1].wait()
    turns = (2, 1, -1, 0)
    for k in (0, 1, 2, 3):
        xb_out[k] = term_b(turns[k], 1 - x).astype(BF)
        start(cross(k))
        if k > 0:
            fold(k - 1)
        if k == 0:
            loads[2].wait()
            loads[3].wait()
            for x_at in (1 - x, x):
                far_a[x_at] = term_a(2, x_at).astype(BF)
                for way in (0, 1):
                    start(far_piece(way, x_at))
    cross(0).wait_recv()
    far_b[...] = (term_b(2, x) + xb_in[0].astype(F32)).astype(BF)
    for way in (0, 1):
        start(far_piece_b(way))
    for x_at in (1 - x, x):
        for way in (0, 1):
            total = term_a(1 - 2 * way, x_at)
            far_piece(way, x_at).wait_recv()
            lo, hi = total[:, :A_HALF], total[:, A_HALF:]
            held = half_a[way, x_at].astype(F32)
            if way == 0:
                lo = lo + held
            else:
                hi = hi + held
            near_a[way, x_at, :, first_a] = lo.astype(BF)
            near_a[way, x_at, :, second_a] = hi.astype(BF)
            start(near_piece(way, x_at))
    fold(3)
    for way in (0, 1):
        total = term_b(1 - 2 * way, x)
        cross(1 + way).wait_recv()
        total = total + xb_in[1 + way].astype(F32)
        far_piece_b(way).wait_recv()
        lo, hi = total[:, :B_HALF], total[:, B_HALF:]
        held = half_b[way].astype(F32)
        if way == 0:
            lo = lo + held
        else:
            hi = hi + held
        near_b[way, :, first_b] = lo.astype(BF)
        near_b[way, :, second_b] = hi.astype(BF)
        start(near_piece_b(way))
    fold(4)
    total = term_a(0, 1 - x)
    for way in (0, 1):
        near_piece(way, 1 - x).wait_recv()
        total = total + got_a[way, 1 - x].astype(F32)
    xa_out[...] = total.astype(BF)
    start(cross_last())
    fold(5)
    sums_ref[...] = tally[6]
    sums_ref[4:5] = came[5, 3:4]
    total = term_b(0, x)
    cross(3).wait_recv()
    total = total + xb_in[3].astype(F32)
    for way in (0, 1):
        near_piece_b(way).wait_recv()
        total = total + got_b[way].astype(F32)
    done[:, pl.ds(A_COLS, B_COLS)] = total
    total = term_a(0, x)
    for way in (0, 1):
        near_piece(way, x).wait_recv()
        total = total + got_a[way, x].astype(F32)
    cross_last().wait_recv()
    done[:, pl.ds(0, A_COLS)] = total + xa_in[...].astype(F32)

    def half(at):
        return done.at[pl.ds(pl.multiple_of(at * 128, 128), 128)]

    give = remote(half(1 - core), out.at[core], ss, sr, me.sibling)
    give.start()
    keep = pltpu.make_async_copy(half(core), out.at[core], osem)
    keep.start()
    keep.wait()
    give.wait_send()
    remote(half(1 - core), out.at[1 - core], ss, sr, me.sibling).wait_recv()
    for copy in sent:
        copy.wait_send()


def weight_gradients(normed, gproj, grads, hcat, sums_a, sums_b):
    dma = pltpu.SemaphoreType.DMA
    rows = 4 * SLOT
    return pl.pallas_call(
        weights_kernel,
        out_shape=(jax.ShapeDtypeStruct((2, 128, COLS), F32), jax.ShapeDtypeStruct((8, D), F32)),
        in_specs=[pl.BlockSpec(memory_space=pl.ANY)] * 4 + [pl.BlockSpec(memory_space=pltpu.VMEM)] * 2,
        out_specs=[pl.BlockSpec(memory_space=pl.ANY), pl.BlockSpec(memory_space=pltpu.VMEM)],
        scratch_shapes=[
            pltpu.VMEM((rows, D), BF),
            pltpu.VMEM((rows, A_COLS), BF),
            pltpu.VMEM((rows, D), BF),
            pltpu.VMEM((rows, B_COLS), BF),
            pltpu.VMEM((4, 256, B_COLS), BF),
            pltpu.VMEM((4, 256, B_COLS), BF),
            pltpu.VMEM((2, 256, A_COLS), BF),
            pltpu.VMEM((256, B_COLS), BF),
            pltpu.VMEM((2, 2, 256, A_HALF), BF),
            pltpu.VMEM((2, 256, B_HALF), BF),
            pltpu.VMEM((2, 2, 256, A_COLS), BF),
            pltpu.VMEM((2, 256, B_COLS), BF),
            pltpu.VMEM((2, 2, 256, A_COLS), BF),
            pltpu.VMEM((2, 256, B_COLS), BF),
            pltpu.VMEM((256, A_COLS), BF),
            pltpu.VMEM((256, A_COLS), BF),
            pltpu.VMEM((256, COLS), F32),
            pltpu.VMEM((7, 8, D), F32),
            pltpu.VMEM((6, 8, D), F32),
            dma((4,)),
            dma((5,)),
            dma((5,)),
            dma((2, 3)),
            dma((2, 3)),
            dma((2, 3)),
            dma((2, 3)),
            dma,
            dma,
            dma,
            dma((6,)),
            dma((6,)),
        ],
        compiler_params=pltpu.CompilerParams(
            collective_id=3, has_side_effects=True, vmem_limit_bytes=60 * MIB
        ),
        name="weight_gradients",
    )(normed.reshape(rows, D), gproj.reshape(rows, A_COLS), grads.reshape(rows, D), hcat.reshape(rows, B_COLS), sums_a, sums_b)


def shards(
    inputs,
    cotangent,
    doc_split,
    qkv_weight,
    qkv_bias,
    out_weight,
    out_bias,
    fc1_weight,
    fc1_bias,
    fc2_weight,
    fc2_bias,
    ln_gain,
    ln_bias,
):
    core = lax.rem(lax.axis_index("dp"), 2)
    block = jnp.concatenate(
        [
            qkv_weight[0].reshape(128, 3, 2, MIX).transpose(2, 0, 1, 3).reshape(2, 128, QKV),
            fc1_weight[0].reshape(128, 2, UP).transpose(1, 0, 2),
            out_weight[0].reshape(2, MIX, 128).transpose(0, 2, 1),
            fc2_weight[0].reshape(2, UP, 128).transpose(0, 2, 1),
        ],
        axis=2,
    )
    mine = jnp.zeros((8, 128), jnp.int32).at[0:2].set(jnp.broadcast_to(doc_split, (2, 128)))
    bias_a = jnp.concatenate(
        [
            lax.dynamic_slice_in_dim(qkv_bias[0], core * MIX, MIX, 1).reshape(1, QKV),
            lax.dynamic_slice_in_dim(fc1_bias[0], core * UP, UP, 0).reshape(1, UP),
        ],
        axis=1,
    )
    bias_b = out_bias + fc2_bias
    w, theirs = gather_weights(block, mine)
    layer_out, input_grad, normed, hcat, grads, gproj, sums_a, sums_b = middle(
        inputs[:, 0], cotangent[:, 0], w, bias_a, bias_b, ln_gain, ln_bias, mine, theirs
    )
    total, sums = weight_gradients(normed, gproj, grads, hcat, sums_a, sums_b)
    sums_a = jnp.where(core == 0, sums[3:5], sums[4:2:-1])[:, 0:A_COLS]
    grad_qkv = total[:, :, 0:QKV].reshape(2, 128, 3, MIX).transpose(1, 2, 0, 3).reshape(128, 3, 2 * MIX)
    grad_fc1 = total[:, :, QKV:A_COLS].transpose(1, 0, 2).reshape(128, 2 * UP)
    grad_out = total[:, :, A_COLS : A_COLS + MIX].transpose(0, 2, 1).reshape(2 * MIX, 128)
    grad_fc2 = total[:, :, A_COLS + MIX :].transpose(0, 2, 1).reshape(2 * UP, 128)
    qkv_bias_grad = sums_a[:, 0:QKV].reshape(2, 3, MIX).transpose(1, 0, 2).reshape(3, 2 * MIX)
    fc1_bias_grad = sums_a[:, QKV:].reshape(2 * UP)
    return (
        layer_out[None, :, None],
        input_grad[None, :, None],
        grad_qkv[None],
        qkv_bias_grad[None],
        grad_out[None],
        sums[2][None],
        grad_fc1[None],
        fc1_bias_grad[None],
        grad_fc2[None],
        sums[2][None],
        sums[0][None],
        sums[1][None],
    )


def solution(mesh):
    rows = P(None, "dp", "tensor", None)
    placed_weights = (
        P("section", "dp", None, "tensor"),
        P("section", None, "tensor"),
        P("section", "tensor", "dp"),
        P("section", None),
        P("section", "dp", "tensor"),
        P("section", "tensor"),
        P("section", "tensor", "dp"),
        P("section", None),
        P("section", None),
        P("section", None),
    )
    out_rows = P("section", None, "dp", "tensor", None)
    return jax.shard_map(
        shards,
        mesh=mesh,
        in_specs=(rows, rows, P(None, "dp")) + placed_weights,
        out_specs=(out_rows, out_rows) + placed_weights,
        check_vma=False,
    )
```

time: 1200 us -> 441 us (0.37); the launches traced: 1190 us -> 441 us
  waiting for transfers between devices: 458 us -> 0 us
  Pallas kernels: 0 us -> 414 us
  blocking collectives: 332 us -> 0 us
  local copies, waits for them, and re-layouts: 151 us -> 21.6 us
  matrix products: 128 us -> 0 us
  other arithmetic: 87.5 us -> 4.08 us
  between operations: 15.6 us -> 0.83 us
  starting transfers between devices: 14.4 us -> 0 us
    pallas_call x0 -> x3, Pallas kernels: none -> 414 us  [the longest x1 204 us: middle(): pl.pallas_call(middle_kernel, out_shape=(jax.ShapeDtypeStruct((2, ROWS, D...]
    psum x2 -> x0, blocking collectives: 332 us -> none  [the longest x1 278 us: shards(): lax.psum((gain_total, shift_total, outbias_total), ('dp', 'tensor'))]
    all_gather x10 -> x0, waiting for transfers between devices: 290 us -> none  [the longest x1 63 us: shards(): lax.all_gather(fc2_weight[0], 'dp', axis=1, tiled=True)]
    reduce_scatter x8 -> x0, waiting for transfers between devices: 143 us -> none  [the longest x3 99.5 us: shards(): lax.psum_scatter(partial_grad.astype(jnp.bfloat16), 'tensor', scatter_dim...]
    dot_general x38 -> x0, matrix products: 128 us -> none  [the longest x2 19.7 us: output_terms(): jnp.einsum('sf,sd->fd', kept_store[6][micro], rows_here, preferred_elemen...]
    unnamed x121 -> x20, local copies, waits for them, and re-layouts: 44.7 us -> 8.41 us
    dynamic_update_slice x38 -> x0, other arithmetic: 34.3 us -> none  [place_slot(): lax.dynamic_update_index_in_dim(buffer, jnp.where(active, value, pick_slo...]
    cond x102 -> x0, local copies, waits for them, and re-layouts: 29 us -> none  [the longest x7 12.8 us: shards(): lax.cond(active, forward_local, spare_forward, normed, split_at)]
  transfers between devices with their start and end apart: 24 -> 0, of which waited for: 16 -> 0; matrix products, arithmetic and copies ran while one was open for 18% -> 0% of each run, Pallas kernels for 0% -> 0%
where the time goes in v1:
time: 441 us
  Pallas kernels  414 us (94%)
  local copies, waits for them, and re-layouts  21.6 us (5%)
    pallas_call x1, Pallas kernels, middle(): pl.pallas_call(middle_kernel, out_shape=(jax.ShapeDtypeStruct((2, ROWS, D...  204 us
    pallas_call x1, Pallas kernels, gather_weights(): pl.pallas_call(gather_kernel, out_shape=(jax.ShapeDtypeStruct((D, COLS),...  111 us
    pallas_call x1, Pallas kernels, weight_gradients(): pl.pallas_call(weights_kernel, out_shape=(jax.ShapeDtypeStruct((2, 128, C...  99.6 us

profile of v1, /device:TPU:1, one launch (start us, length us, event | category | flops | bytes accessed | tf_op | source)
XLA Modules:
  0.0 440.6 jit_solution(5261008203387083922)
XLA Ops:
  0.7 0.7 scatter.7
  1.4 0.7 constant_dynamic-slice_fusion.1
  2.1 0.7 scatter.8.split.mine_ref
  3.4 1.3 add.15.bb_ref
  4.7 1.0 copy.48
  5.7 1.2 copy.44
  7.1 1.3 copy.46
  8.9 1.3 pad_maximum_fusion.block
  10.2 110.8 %gather_weights.1 = (bf16[2048,3072]{1,0:T(8,128)(2,1)}, s32[8,128]{1,0:T(8,128)}) custom-call(bf16[2,128,3072]{2,1,0:T(8,128)(2,1)} %pad_maximum_fusion.block, s32[8,128]{1,0:T(8,128)} %scatter.8.split.mine_ref), custom_call_target="tpu_custom_call" | custom-call | tf_op jit(solution)/shard_map/gather_weights/pallas_call | solution.py:178
  121.0 203.7 %both_layers.1 = (bf16[2,64,2048]{2,1,0:T(8,128)(2,1)}, bf16[2,64,2048]{2,1,0:T(8,128)(2,1)}, bf16[4,256,2048]{2,1,0:T(8,128)(2,1)}, bf16[4,256,1280]{2,1,0:T(8,...) custom-call(bf16[2,64,2048]{2,1,0:T(8,128)(2,1)} %bitcast.57, ...), custom_call_target="tpu_custom_call" | custom-call | tf_op jit(solution)/shard_map/both_layers/pallas_call | solution.py:569
  324.7 99.6 %weight_gradients.1 = (f32[2,128,3072]{2,1,0:T(8,128)}, f32[8,2048]{1,0:T(8,128)}) custom-call(bf16[1024,2048]{1,0:T(8,128)(2,1)} %bitcast.45, bf16[1024,1792]{1,0:T(8,128)(2,1)} %bitcast.47, bf16[1024,2048]{1,0:T(8,128)(2,1)} %bitcast.46, bf16[1024,1280]{1,0:T(8,128)(2,1)} %bitcast.50, f32[8,1792]{1,0:T(8,128)} %get-tuple-element.44.sa_ref, ...), custom_call_target="tpu_custom_call" | custom-call | tf_op jit(solution)/shard_map/weight_gradients/pallas_call | solution.py:789
  424.3 0.8 slice.52
  425.6 0.9 broadcast_select_fusion
  426.5 1.6 fusion
  428.0 0.6 copy.61
  429.3 1.0 slice_bitcast_fusion.2
  430.2 0.8 copy.53
  431.1 1.2 slice.51
  432.3 1.7 slice_bitcast_fusion
  433.9 1.3 copy.55
  435.6 1.1 copy.58
  437.1 1.3 copy.60
  439.0 0.8 copy.66
  439.8 0.8 copy.67
  (25 shorter events, 3.6 us)
Async XLA Ops:
  0.6 2.1 copy-start
  0.7 8.0 %copy-start.1 = (bf16[1,2048,128]{2,1,0:T(8,128)(2,1)S(1)}, bf16[1,2048,128]{2,1,0:T(8,128)(2,1)}, u32[]{:S(2)}) copy-start(bf16[1,2048,128]{2,1,0:T(8,128)(2,1)} %param.26) | copy-start | bytes 1572868
  428.0 10.4 %copy-start.4 = (f32[1,2048]{1,0:T(1,128)}, f32[1,2048]{1,0:T(1,128)S(1)}, u32[]{:S(2)}) copy-start(f32[1,2048]{1,0:T(1,128)S(1)} %get-tuple-element.130) | copy-start | bytes 24580
  435.6 3.4 copy-start.3
  435.6 4.2 copy-start.2

commit v2 on v1

--- a/solution.py
+++ b/solution.py
@@ -77,136 +77,118 @@
         return {"tensor": lax.rem(self.z + by, 4)}
 
 
-def gather_kernel(block, split, w, their_split, own_sem, x_send, x_recv, y_send, y_recv, sib_send, sib_recv):
-    me = Place()
-    greet([me.sibling, me.across, me.beside(1), me.beside(-1)])
-
-    def rows(dp):
-        return pl.ds(pl.multiple_of(dp * 128, 128), 128)
-
-    def chip(y, x):
-        return pl.ds(pl.multiple_of((y * 2 + x) * 256, 256), 256)
-
-    other = me.dp + 1 - 2 * me.core
-    keep = pltpu.make_async_copy(block.at[me.core], w.at[rows(me.dp)], own_sem)
-    keep.start()
-    give = remote(block.at[1 - me.core], w.at[rows(me.dp)], sib_send.at[0], sib_recv.at[0], me.sibling)
-    give.start()
-    tell = remote(split, their_split, sib_send.at[1], sib_recv.at[1], me.sibling)
-    tell.start()
-    keep.wait()
-    remote(block.at[1 - me.core], w.at[rows(other)], sib_send.at[0], sib_recv.at[0], me.sibling).wait_recv()
-
-    cols = [
-        pl.ds(0, A_HALF),
-        pl.ds(A_HALF, A_HALF),
-        pl.ds(A_COLS, B_HALF),
-        pl.ds(A_COLS + B_HALF, B_HALF),
-    ]
-
-    def part(y, x, which):
-        return w.at[chip(y, x), cols[which]]
-
-    def over_x(y, x, which, slot):
-        piece = part(y, x, which)
-        return remote(piece, piece, x_send.at[slot], x_recv.at[slot], me.across)
-
-    def over_y(by, y, x, which, slot):
-        piece = part(y, x, which)
-        way = 0 if by > 0 else 1
-        return remote(piece, piece, y_send.at[way, slot], y_recv.at[way, slot], me.beside(by))
-
-    sent = []
-
-    def start(copy):
-        copy.start()
-        sent.append(copy)
-
-    y, x = me.y, me.x
-    for which in (0, 1):
-        start(over_x(y, x, which, which))
-    for which in (2, 3):
-        for by in (1, -1):
-            start(over_y(by, y, x, which, which))
-    for which in (2, 3):
-        start(over_x(y, x, which, which))
-    for which in (0, 1):
-        for by in (1, -1):
-            start(over_y(by, y, x, which, which))
-    for which in (2, 3):
-        for by in (1, -1):
-            source = me.turn(-by)
-            over_y(by, source, x, which, which).wait_recv()
-            if (which == 2) == (by > 0):
-                start(over_y(by, source, x, which, 6))
-            start(over_x(source, x, which, 2 * which + (0 if by > 0 else 1)))
-    for which in (0, 1):
-        over_x(y, 1 - x, which, which).wait_recv()
-        for by in (1, -1):
-            start(over_y(by, y, 1 - x, which, 4 + which))
-    far = me.turn(2)
-    for which, by in ((2, 1), (3, -1)):
-        over_y(by, far, x, which, 6).wait_recv()
-        start(over_x(far, x, which, 6 + which))
-    for which, by in ((0, 1), (1, -1)):
-        source = me.turn(-by)
-        over_y(by, source, x, which, which).wait_recv()
-        start(over_y(by, source, x, which, 7))
-    for which, by in ((0, 1), (1, -1)):
-        source = me.turn(-by)
-        over_y(by, source, 1 - x, which, 4 + which).wait_recv()
-        start(over_y(by, source, 1 - x, which, 8))
-    for which, by in ((0, -1), (1, 1)):
-        source = me.turn(-by)
-        over_y(by, source, x, which, which).wait_recv()
-        over_y(by, source, 1 - x, which, 4 + which).wait_recv()
-    for which in (2, 3):
-        over_x(y, 1 - x, which, which).wait_recv()
-        for by in (1, -1):
-            over_x(me.turn(-by), 1 - x, which, 2 * which + (0 if by > 0 else 1)).wait_recv()
-        over_x(far, 1 - x, which, 6 + which).wait_recv()
-    for which, by in ((0, 1), (1, -1)):
-        over_y(by, far, x, which, 7).wait_recv()
-        over_y(by, far, 1 - x, which, 8).wait_recv()
-    for copy in sent:
-        copy.wait_send()
-    give.wait_send()
-    tell.wait()
-
-
-def gather_weights(block, split):
-    return pl.pallas_call(
-        gather_kernel,
-        out_shape=(jax.ShapeDtypeStruct((D, COLS), BF), jax.ShapeDtypeStruct(split.shape, split.dtype)),
-        in_specs=[pl.BlockSpec(memory_space=pl.ANY)] * 2,
-        out_specs=[pl.BlockSpec(memory_space=pl.ANY)] * 2,
-        scratch_shapes=[
-            pltpu.SemaphoreType.DMA,
-            pltpu.SemaphoreType.DMA((10,)),
-            pltpu.SemaphoreType.DMA((10,)),
-            pltpu.SemaphoreType.DMA((2, 9)),
-            pltpu.SemaphoreType.DMA((2, 9)),
-            pltpu.SemaphoreType.DMA((2,)),
-            pltpu.SemaphoreType.DMA((2,)),
-        ],
-        compiler_params=pltpu.CompilerParams(collective_id=1, has_side_effects=True),
-        name="gather_weights",
-    )(block, split)
-
-
-def middle_kernel(
-    x_ref, cot_ref, w_hbm, ba_ref, bb_ref, gain_ref, shift_ref, mine_ref, theirs_ref, cos_ref, sin_ref,
+STAGES = (
+    ((0, 512), (512, 512), (1024, 384), (1408, 384)),
+    ((1792, 384), (2176, 384), (2560, 256), (2816, 256)),
+)
+
+
+def layers_kernel(
+    x_ref, cot_ref, block, qb_ref, ub_ref, ob_ref, db_ref, gain_ref, shift_ref, mine_ref, cos_ref, sin_ref,
     lo_ref, ig_ref, n_out, h_out, g_out, p_out, sa_ref, sb_ref,
-    w, normed, grads, qkv, hcat, slope, probs, gproj, part, got, zgot, xrow, grow, ctab, stab, split,
-    wsem, agz_s, agz_r, ags_s, ags_r, par_s, par_r, rsz_s, rsz_r, sec_s, sec_r, osem,
+    w, normed, grads, qkv, hcat, slope, probs, gproj, part, got, zgot, xrow, grow, ctab, stab, split, theirs, bias,
+    own_sem, x_send, x_recv, y_send, y_recv, sib_send, sib_recv,
+    agz_s, agz_r, ags_s, ags_r, par_s, par_r, rsz_s, rsz_r, sec_s, sec_r, osem,
 ):
     me = Place()
     section = lax.axis_index("section")
     core, z = me.core, me.z
-    greet([me.z_peer(1), me.z_peer(2), me.z_peer(3), me.sibling, {"section": 1 - section}])
-
-    load_a = pltpu.make_async_copy(w_hbm.at[:, pl.ds(0, A_COLS)], w.at[:, pl.ds(0, A_COLS)], wsem.at[0])
-    load_b = pltpu.make_async_copy(w_hbm.at[:, pl.ds(A_COLS, B_COLS)], w.at[:, pl.ds(A_COLS, B_COLS)], wsem.at[1])
+    greet(
+        [me.sibling, me.across, me.beside(1), me.beside(-1)]
+        + [me.z_peer(1), me.z_peer(2), me.z_peer(3), {"section": 1 - section}]
+    )
+
+    def rows(dp):
+        return pl.ds(pl.multiple_of(dp * 128, 128), 128)
+
+    def chip(y_at, x_at):
+        return pl.ds(pl.multiple_of((y_at * 2 + x_at) * 256, 256), 256)
+
+    other = me.dp + 1 - 2 * core
+    hold = pltpu.make_async_copy(block.at[core], w.at[rows(me.dp)], own_sem)
+    give = remote(block.at[1 - core], w.at[rows(me.dp)], sib_send.at[0], sib_recv.at[0], me.sibling)
+    take = remote(block.at[1 - core], w.at[rows(other)], sib_send.at[0], sib_recv.at[0], me.sibling)
+    tell = remote(mine_ref, theirs, sib_send.at[1], sib_recv.at[1], me.sibling)
+    y, x = me.y, me.x
+    far = me.turn(2)
+
+    def piece_of(stage, y_at, x_at, which):
+        return w.at[chip(y_at, x_at), pl.ds(*STAGES[stage][which])]
+
+    def over_x(stage, y_at, x_at, which, slot):
+        piece = piece_of(stage, y_at, x_at, which)
+        return remote(piece, piece, x_send.at[stage, slot], x_recv.at[stage, slot], me.across)
+
+    def over_y(stage, by, y_at, x_at, which, slot):
+        piece = piece_of(stage, y_at, x_at, which)
+        way = 0 if by > 0 else 1
+        return remote(piece, piece, y_send.at[stage, way, slot], y_recv.at[stage, way, slot], me.beside(by))
+
+    sent = []
+
+    def start(copy):
+        copy.start()
+        sent.append(copy)
+
+    def own_first(stage):
+        for which in (0, 1):
+            start(over_x(stage, y, x, which, which))
+        for which in (2, 3):
+            for by in (1, -1):
+                start(over_y(stage, by, y, x, which, which))
+
+    def own_second(stage):
+        for which in (2, 3):
+            start(over_x(stage, y, x, which, which))
+        for which in (0, 1):
+            for by in (1, -1):
+                start(over_y(stage, by, y, x, which, which))
+
+    def pass_near(stage):
+        for which in (2, 3):
+            for by in (1, -1):
+                source = me.turn(-by)
+                over_y(stage, by, source, x, which, which).wait_recv()
+                if (which == 2) == (by > 0):
+                    start(over_y(stage, by, source, x, which, 6))
+                start(over_x(stage, source, x, which, 2 * which + (0 if by > 0 else 1)))
+
+    def pass_crossed(stage):
+        for which in (0, 1):
+            over_x(stage, y, 1 - x, which, which).wait_recv()
+            for by in (1, -1):
+                start(over_y(stage, by, y, 1 - x, which, 4 + which))
+
+    def pass_far(stage):
+        for which, by in ((2, 1), (3, -1)):
+            over_y(stage, by, far, x, which, 6).wait_recv()
+            start(over_x(stage, far, x, which, 6 + which))
+
+    def pass_on(stage):
+        for which, by in ((0, 1), (1, -1)):
+            source = me.turn(-by)
+            over_y(stage, by, source, x, which, which).wait_recv()
+            start(over_y(stage, by, source, x, which, 7))
+
+    def pass_on_crossed(stage):
+        for which, by in ((0, 1), (1, -1)):
+            source = me.turn(-by)
+            over_y(stage, by, source, 1 - x, which, 4 + which).wait_recv()
+            start(over_y(stage, by, source, 1 - x, which, 8))
+
+    def settle(stage):
+        for which, by in ((0, -1), (1, 1)):
+            source = me.turn(-by)
+            over_y(stage, by, source, x, which, which).wait_recv()
+            over_y(stage, by, source, 1 - x, which, 4 + which).wait_recv()
+        for which in (2, 3):
+            over_x(stage, y, 1 - x, which, which).wait_recv()
+            for by in (1, -1):
+                over_x(stage, me.turn(-by), 1 - x, which, 2 * which + (0 if by > 0 else 1)).wait_recv()
+            over_x(stage, far, 1 - x, which, 6 + which).wait_recv()
+        for which, by in ((0, 1), (1, -1)):
+            over_y(stage, by, far, x, which, 7).wait_recv()
+            over_y(stage, by, far, 1 - x, which, 8).wait_recv()
 
     def band(at):
         return pl.ds(pl.multiple_of(at * ROWS, ROWS), ROWS)
@@ -294,7 +276,7 @@
 
     def finish_forward(i):
         m = i // 2
-        lo_ref[m] = (xrow[m].astype(F32) + row_sum(0, i) + bb_ref[...]).astype(BF)
+        lo_ref[m] = (xrow[m].astype(F32) + row_sum(0, i) + (ob_ref[...] + db_ref[...])).astype(BF)
 
         @pl.when(section == 0)
         def _():
@@ -333,7 +315,7 @@
 
     def forward_first(i):
         rows = normed[i]
-        projected = dot(rows, w[:, 0:QKV]) + ba_ref[0:1, 0:QKV]
+        projected = dot(rows, w[:, 0:QKV]) + bias[0:1, 0:QKV]
         queries = turned(projected[:, 0:MIX], i, 1.0).astype(BF)
         keys = turned(projected[:, MIX : 2 * MIX], i, 1.0).astype(BF)
         values = projected[:, 2 * MIX : 3 * MIX].astype(BF)
@@ -355,7 +337,7 @@
             probs[i, head] = chances
             mixed = mixed + dot(chances, values * mask)
         hcat[i, :, 0:MIX] = mixed.astype(BF)
-        v = dot(rows, w[:, QKV:A_COLS]) + ba_ref[0:1, QKV:A_COLS]
+        v = dot(rows, w[:, QKV:A_COLS]) + bias[0:1, QKV:A_COLS]
         root = np.sqrt(2 / np.pi).astype(np.float32)
         square = v * v
         bent = jnp.tanh(root * (v + 0.044715 * (square * v)))
@@ -405,10 +387,15 @@
         source, target = ((normed, n_out), (hcat, h_out), (grads, g_out), (gproj, p_out))[which]
         return pltpu.make_async_copy(source.at[i], target.at[i], osem.at[which, i])
 
-    load_a.start()
-    load_b.start()
+    hold.start()
+    give.start()
+    tell.start()
     sa_ref[...] = jnp.zeros_like(sa_ref)
     sb_ref[...] = jnp.zeros_like(sb_ref)
+    hold.wait()
+    take.wait_recv()
+    own_first(0)
+    own_second(0)
 
     @pl.when(section == 0)
     def _():
@@ -422,10 +409,16 @@
         for m in range(2):
             spread_own(1, m)
 
+    for at in range(3):
+        bias[0:1, at * MIX : (at + 1) * MIX] = jnp.where(
+            core == 0, qb_ref[at : at + 1, 0:MIX], qb_ref[at : at + 1, MIX : 2 * MIX]
+        )
+    bias[0:1, QKV:A_COLS] = jnp.where(core == 0, ub_ref[0:1, 0:UP], ub_ref[0:1, UP : 2 * UP])
+    tell.wait_recv()
     places = lax.broadcasted_iota(jnp.int32, (SLOT, 128), 0)
     sign = jnp.where(early, -1.0, 1.0)
     for i in range(4):
-        at = jnp.where(core == i % 2, mine_ref[i // 2 : i // 2 + 1, :], theirs_ref[i // 2 : i // 2 + 1, :])
+        at = jnp.where(core == i % 2, mine_ref[i // 2 : i // 2 + 1, :], theirs[i // 2 : i // 2 + 1, :])
         split[i : i + 1, :] = at
         first = places < at
         here = places == at
@@ -435,65 +428,105 @@
         ctab[i] = jnp.where(first, cosine, cosine * cos_at + sine * sin_at)
         stab[i] = jnp.where(first, sine, sine * cos_at - cosine * sin_at) * sign
 
-    @pl.when((section == 1) & (core == 0))
-    def _():
-        onward(0, 0).wait_recv()
-        spread_own(0, 0)
-
-    @pl.when(core == 0)
-    def _():
-        relay(0, 0)
-
-    load_a.wait()
-    load_b.wait()
-
-    def forward_step(i, _):
-        own = lax.rem(i, 2) == core
-
-        @pl.when((section == 1) & (i < 3) & jnp.logical_not(own))
-        def _():
-            onward(0, (i + 1) // 2).wait_recv()
-            spread_own(0, (i + 1) // 2)
-
-        @pl.when(i < 4)
+    pass_near(0)
+    pass_crossed(0)
+
+    def relay_early(m):
+        @pl.when(section == 0)
+        def _():
+            relay(0, 2 * m + core)
+
+        @pl.when(section == 1)
+        def _():
+            relay(1, 2 * m + core)
+
+    relay_early(0)
+    pass_on(0)
+    own_first(1)
+    pass_far(0)
+    relay_early(1)
+    pass_on_crossed(0)
+    own_second(1)
+    settle(0)
+    pass_near(1)
+
+    def forward_early(i):
+        @pl.when(section == 0)
         def _():
             await_rows(0, i)
             forward_first(i)
 
-        @pl.when((i < 3) & jnp.logical_not(own))
-        def _():
-            relay(0, i + 1)
-
-        @pl.when((i >= 1) & (i < 5) & jnp.logical_not(own))
-        def _():
-            pair_sum(0, i - 1)
-
-        @pl.when((i >= 2) & own)
-        def _():
-            finish_forward(i - 2)
-
-        @pl.when(i < 4)
-        def _():
-            forward_second(i)
-            keep(0, i).start()
-            keep(1, i).start()
-
-            @pl.when(jnp.logical_not(own))
+    forward_early(0)
+    pass_crossed(1)
+    forward_early(1)
+    pass_on(1)
+    pass_far(1)
+    forward_early(2)
+    forward_early(3)
+    pass_on_crossed(1)
+    settle(1)
+
+    def forward_last(i):
+        forward_second(i)
+        keep(0, i).start()
+        keep(1, i).start()
+
+        @pl.when(lax.rem(i, 2) != core)
+        def _():
+            to_pair(0, i).start()
+
+    def finish_forward_all():
+        for m in range(2):
+            finish_forward(2 * m + core)
+
+    @pl.when(section == 0)
+    def _():
+        def step(i, _):
+            forward_last(i)
+
+            @pl.when(i == 1 + core)
             def _():
-                to_pair(0, i).start()
-
-        return 0
-
-    lax.fori_loop(0, 6, forward_step, 0)
-
-    @pl.when((section == 0) & (core == 0))
+                pair_sum(0, core)
+
+            return 0
+
+        lax.fori_loop(0, 4, step, 0)
+        pair_sum(0, 2 + core)
+        finish_forward_all()
+
+        @pl.when(core == 0)
+        def _():
+            onward(1, 0).wait_recv()
+            spread_own(1, 0)
+            relay(1, 0)
+
+    @pl.when(section == 1)
     def _():
-        onward(1, 0).wait_recv()
-        spread_own(1, 0)
-
-    @pl.when(core == 0)
-    def _():
-        relay(1, 0)
+        @pl.when(core == 0)
+        def _():
+            onward(0, 0).wait_recv()
+            spread_own(0, 0)
+            relay(0, 0)
+
+        def step(i, _):
+            own = lax.rem(i, 2) == core
+
+            @pl.when((i < 3) & jnp.logical_not(own))
+            def _():
+                onward(0, (i + 1) // 2).wait_recv()
+                spread_own(0, (i + 1) // 2)
+
+            await_rows(0, i)
+            forward_first(i)
+
+            @pl.when((i < 3) & jnp.logical_not(own))
+            def _():
+                relay(0, i + 1)
+
+            forward_last(i)
+            return 0
+
+        lax.fori_loop(0, 4, step, 0)
 
     def backward_step(i, _):
         own = lax.rem(i, 2) == core
@@ -508,7 +541,7 @@
             await_rows(1, i)
             backward_first(i)
 
-        @pl.when((i < 3) & jnp.logical_not(own))
+        @pl.when((section == 0) & (i < 3) & jnp.logical_not(own))
         def _():
             relay(1, i + 1)
 
@@ -534,6 +567,16 @@
 
     lax.fori_loop(0, 6, backward_step, 0)
 
+    @pl.when(section == 1)
+    def _():
+        for m in range(2):
+            pair_sum(0, 2 * m + core)
+        finish_forward_all()
+
+    for copy in sent:
+        copy.wait_send()
+    give.wait_send()
+    tell.wait_send()
     for back in range(2):
         for m in range(2):
             mine = 2 * m + core
@@ -554,7 +597,7 @@
             keep(which, i).wait()
 
 
-def middle(rows_in, cotangent, w, bias_a, bias_b, gain, shift, mine, theirs):
+def both_layers(rows_in, cotangent, block, bias_qkv, bias_up, bias_out, bias_down, gain, shift, mine):
     places = np.arange(SLOT, dtype=np.float32)
     frequency = (10000.0 ** (-(np.arange(ROT // 2, dtype=np.float32) * np.float32(2.0 / ROT)))).astype(np.float32)
     angles = (places[:, None] * frequency[None, :]).astype(np.float32).astype(np.float64)
@@ -567,7 +610,7 @@
     vmem = pl.BlockSpec(memory_space=pltpu.VMEM)
     dma = pltpu.SemaphoreType.DMA
     return pl.pallas_call(
-        middle_kernel,
+        layers_kernel,
         out_shape=(
             jax.ShapeDtypeStruct((2, ROWS, D), BF),
             jax.ShapeDtypeStruct((2, ROWS, D), BF),
@@ -578,7 +621,7 @@
             jax.ShapeDtypeStruct((8, A_COLS), F32),
             jax.ShapeDtypeStruct((8, D), F32),
         ),
-        in_specs=[vmem, vmem, any_] + [vmem] * 8,
+        in_specs=[vmem, vmem, any_] + [vmem] * 9,
         out_specs=[vmem, vmem] + [any_] * 4 + [vmem, vmem],
         scratch_shapes=[
             pltpu.VMEM((D, COLS), BF),
@@ -597,6 +640,14 @@
             pltpu.VMEM((4, SLOT, 128), F32),
             pltpu.VMEM((4, SLOT, 128), F32),
             pltpu.VMEM((8, 128), jnp.int32),
+            pltpu.VMEM((8, 128), jnp.int32),
+            pltpu.VMEM((8, A_COLS), F32),
+            dma,
+            dma((2, 10)),
+            dma((2, 10)),
+            dma((2, 2, 9)),
+            dma((2, 2, 9)),
+            dma((2,)),
             dma((2,)),
             dma((2, 2, 3)),
             dma((2, 2, 3)),
@@ -614,7 +665,7 @@
             collective_id=2, has_side_effects=True, vmem_limit_bytes=62 * MIB
         ),
         name="both_layers",
-    )(rows_in, cotangent, w, bias_a, bias_b, gain, shift, mine, theirs, cosine, sine)
+    )(rows_in, cotangent, block, bias_qkv, bias_up, bias_out, bias_down, gain, shift, mine, cosine, sine)
 
 
 def weights_kernel(
@@ -825,7 +876,7 @@
             dma((6,)),
         ],
         compiler_params=pltpu.CompilerParams(
-            collective_id=3, has_side_effects=True, vmem_limit_bytes=60 * MIB
+            collective_id=1, has_side_effects=True, vmem_limit_bytes=60 * MIB
         ),
         name="weight_gradients",
     )(normed.reshape(rows, D), gproj.reshape(rows, A_COLS), grads.reshape(rows, D), hcat.reshape(rows, B_COLS), sums_a, sums_b)
@@ -856,18 +907,18 @@
         ],
         axis=2,
     )
-    mine = jnp.zeros((8, 128), jnp.int32).at[0:2].set(jnp.broadcast_to(doc_split, (2, 128)))
-    bias_a = jnp.concatenate(
-        [
-            lax.dynamic_slice_in_dim(qkv_bias[0], core * MIX, MIX, 1).reshape(1, QKV),
-            lax.dynamic_slice_in_dim(fc1_bias[0], core * UP, UP, 0).reshape(1, UP),
-        ],
-        axis=1,
-    )
-    bias_b = out_bias + fc2_bias
-    w, theirs = gather_weights(block, mine)
-    layer_out, input_grad, normed, hcat, grads, gproj, sums_a, sums_b = middle(
-        inputs[:, 0], cotangent[:, 0], w, bias_a, bias_b, ln_gain, ln_bias, mine, theirs
+    mine = jnp.broadcast_to(doc_split[None], (4, 2, 128)).reshape(8, 128)
+    layer_out, input_grad, normed, hcat, grads, gproj, sums_a, sums_b = both_layers(
+        inputs[:, 0],
+        cotangent[:, 0],
+        block,
+        qkv_bias[0],
+        fc1_bias,
+        out_bias,
+        fc2_bias,
+        ln_gain,
+        ln_bias,
+        mine,
     )
     total, sums = weight_gradients(normed, gproj, grads, hcat, sums_a, sums_b)
     sums_a = jnp.where(core == 0, sums[3:5], sums[4:2:-1])[:, 0:A_COLS]

time: 441 us -> 386 us (0.88)
  the two profiles are of different devices: /device:TPU:1 before, /device:TPU:3 now
where the time goes in v2:
time: 386 us; the launch traced here: 379 us
  Pallas kernels  358 us (93%)
  local copies, waits for them, and re-layouts  19.2 us (5%)
    pallas_call x1, Pallas kernels, both_layers(): pl.pallas_call(layers_kernel, out_shape=(jax.ShapeDtypeStruct((2, ROWS, D...  253 us
    pallas_call x1, Pallas kernels, weight_gradients(): pl.pallas_call(weights_kernel, out_shape=(jax.ShapeDtypeStruct((2, 128, C...  105 us
    unnamed x25, local copies, waits for them, and re-layouts  8.02 us

profile of v2, /device:TPU:3, one launch (start us, length us, event | category | flops | bytes accessed | tf_op | source)
XLA Modules:
  0.0 379.2 jit_solution(16270440954554462261)
XLA Ops:
  0.7 1.3 copy.49
  2.0 1.0 copy.48
  3.0 1.3 copy.46
  5.0 1.4 pad_maximum_fusion.block
  6.4 0.6 copy.64
  7.1 0.7 broadcast_in_dim.21.mine_ref
  7.7 252.9 %both_layers.1 = (bf16[2,64,2048]{2,1,0:T(8,128)(2,1)}, bf16[2,64,2048]{2,1,0:T(8,128)(2,1)}, bf16[4,256,2048]{2,1,0:T(8,128)(2,1)}, bf16[4,256,1280]{2,1,0:T(8,...) custom-call(bf16[2,64,2048]{2,1,0:T(8,128)(2,1)} %bitcast.63, ...), custom_call_target="tpu_custom_call" | custom-call | tf_op jit(solution)/shard_map/both_layers/pallas_call | solution.py:612
  260.6 104.7 %weight_gradients.1 = (f32[2,128,3072]{2,1,0:T(8,128)}, f32[8,2048]{1,0:T(8,128)}) custom-call(bf16[1024,2048]{1,0:T(8,128)(2,1)} %bitcast.47, bf16[1024,1792]{1,0:T(8,128)(2,1)} %bitcast.49, bf16[1024,2048]{1,0:T(8,128)(2,1)} %bitcast.48, bf16[1024,1280]{1,0:T(8,128)(2,1)} %bitcast.52, f32[8,1792]{1,0:T(8,128)} %get-tuple-element.28.sa_ref, ...), custom_call_target="tpu_custom_call" | custom-call | tf_op jit(solution)/shard_map/weight_gradients/pallas_call | solution.py:840
  365.3 1.2 slice.35
  366.5 0.3 copy.51
  366.8 1.1 copy.58
  368.0 0.4 rev.3
  368.5 0.6 copy.59
  369.1 1.0 slice_bitcast_fusion.2
  370.0 0.8 copy.53
  370.9 0.6 fusion
  371.5 1.7 slice_bitcast_fusion
  373.2 0.3 copy.54
  373.5 1.3 copy.60
  374.8 0.6 copy.62
  375.5 1.3 copy.55
  376.8 0.6 copy.68
  377.4 0.8 copy.69
  378.2 0.8 copy.70
  (26 shorter events, 0.9 us)
Async XLA Ops:
  0.6 3.9 %copy-start.2 = (bf16[1,128,3,512]{3,1,2,0:T(8,128)(2,1)S(1)}, bf16[1,128,3,512]{3,1,2,0:T(8,128)(2,1)}, u32[]{:S(2)}) copy-start(bf16[1,128,3,512]{3,1,2,0:T(8,128)(2,1)} %param.18) | copy-start | bytes 1179652
  4.3 2.1 copy-start.5
  4.3 2.7 copy-start.6
  365.3 2.7 copy-start.3
  371.5 5.3 %copy-start.4 = (f32[1,2048]{1,0:T(1,128)}, f32[1,2048]{1,0:T(1,128)S(1)}, u32[]{:S(2)}) copy-start(f32[1,2048]{1,0:T(1,128)S(1)} %get-tuple-element.114) | copy-start | bytes 24580
  373.5 3.9 %copy-start.1 = (bf16[2,64,2048]{2,1,0:T(8,128)(2,1)S(1)}, bf16[2,64,2048]{2,1,0:T(8,128)(2,1)}, u32[]{:S(2)}) copy-start(bf16[2,64,2048]{2,1,0:T(8,128)(2,1)} %get-tuple-element.22) | copy-start | bytes 1572868
  373.5 4.6 %copy-start = (bf16[2,64,2048]{2,1,0:T(8,128)(2,1)S(1)}, bf16[2,64,2048]{2,1,0:T(8,128)(2,1)}, u32[]{:S(2)}) copy-start(bf16[2,64,2048]{2,1,0:T(8,128)(2,1)} %get-tuple-element.23) | copy-start | bytes 1572868

commit v3 on v2

v3 whole, which is shorter than its diff:
```python
from functools import partial

import jax
import jax.numpy as jnp
import numpy as np
from jax import lax
from jax.experimental import pallas as pl
from jax.experimental.pallas import tpu as pltpu
from jax.sharding import PartitionSpec as P

HD = 64
ROT = 32
EPSILON = 1e-05
MESH = pl.DeviceIdType.MESH
BF = jnp.bfloat16
F32 = jnp.float32

D = 2048
SLOT = 256
ROWS = 64
QKV = 768
UP = 1024
A_COLS = QKV + UP
MIX = 256
B_COLS = MIX + UP
A_HALF = A_COLS // 2
B_HALF = B_COLS // 2
ALL = 4 * SLOT
VMEM_LIMIT = 62 * 2**20


def dot(a, b):
    return lax.dot_general(a, b, (((1,), (0,)), ((), ())), preferred_element_type=F32)


def dot_nt(a, b):
    return lax.dot_general(a, b, (((1,), (1,)), ((), ())), preferred_element_type=F32)


def dot_tn(a, b):
    return lax.dot_general(a, b, (((0,), (0,)), ((), ())), preferred_element_type=F32)


def remote(src, dst, send, recv, device):
    return pltpu.make_async_remote_copy(
        src_ref=src, dst_ref=dst, send_sem=send, recv_sem=recv, device_id=device, device_id_type=MESH
    )


def greet(peers):
    barrier = pltpu.get_barrier_semaphore()
    for peer in peers:
        pl.semaphore_signal(barrier, inc=1, device_id=peer, device_id_type=MESH)
    pl.semaphore_wait(barrier, len(peers))


class Place:
    def __init__(self):
        self.dp = lax.axis_index("dp")
        self.core = lax.rem(self.dp, 2)
        self.x = lax.rem(self.dp // 2, 2)
        self.y = self.dp // 4
        self.z = lax.axis_index("tensor")
        self.sibling = {"dp": self.dp + 1 - 2 * self.core}
        self.across = {"dp": self.at(self.y, 1 - self.x, self.core)}

    def at(self, y, x, core):
        return (y * 2 + x) * 2 + core

    def turn(self, by):
        return lax.rem(self.y + 4 + by, 4)

    def beside(self, by):
        return {"dp": self.at(self.turn(by), self.x, self.core)}

    def z_peer(self, by):
        return {"tensor": lax.rem(self.z + by, 4)}


STAGES = (
    ((0, 512), (512, 512), (1024, 384), (1408, 384)),
    ((0, 384), (384, 384), (768, 256), (1024, 256)),
)


def layers_kernel(
    x_hbm, cot_hbm, qkv_hbm, up_hbm, ow_hbm, dw_hbm,
    qb_ref, ub_ref, ob_ref, db_ref, gain_ref, shift_ref, mine_ref, cos_ref, sin_ref,
    lo_out, ig_out, gq_out, gu_out, go_out, gd_out, sums_ref, gqb_ref, gub_ref, aside_out,
    wa, wb, normed, grads, qkv, hcat, slope, probs, gproj, part, got, zgot, xrow, grow, ctab, stab, split, theirs, bias,
    half_a, half_b, got_a, got_b, xa_in, sum_a, tally, came,
    own_sem, x_send, x_recv, y_send, y_recv, sib_send, sib_recv,
    agz_s, agz_r, ags_s, ags_r, par_s, par_r, rsz_s, rsz_r, sec_s, sec_r,
    xs, xr, fs, fr, ns, nr, ts, tr, end_s, end_r, end_k, keep_s, free_sem, pair_free, aside_s,
):
    me = Place()
    section = lax.axis_index("section")
    core, z = me.core, me.z
    greet(
        [me.sibling, me.across, me.beside(1), me.beside(-1), me.beside(2)]
        + [me.z_peer(1), me.z_peer(2), me.z_peer(3), {"section": 1 - section}]
    )

    def device_span(dp):
        return pl.ds(pl.multiple_of(dp * 128, 128), 128)

    def chip_span(y_at, x_at):
        return pl.ds(pl.multiple_of((y_at * 2 + x_at) * 256, 256), 256)

    def place(at, size):
        return pl.ds(pl.multiple_of(at * size, size), size)

    def blocks(dp, half):
        span = device_span(dp)
        pairs = [
            (qkv_hbm.at[k, :, place(half, MIX)], wa.at[span, pl.ds(k * MIX, MIX)]) for k in range(3)
        ]
        pairs.append((up_hbm.at[:, place(half, UP)], wa.at[span, pl.ds(QKV, UP)]))
        pairs.append((ow_hbm.at[place(half, MIX), :], wb.at[pl.ds(0, MIX), span]))
        pairs.append((dw_hbm.at[place(half, UP), :], wb.at[pl.ds(MIX, UP), span]))
        return pairs

    other = me.dp + 1 - 2 * core
    holds = [
        pltpu.make_async_copy(source, target, own_sem.at[at])
        for at, (source, target) in enumerate(blocks(me.dp, core))
    ]
    gives = [
        remote(source, target, sib_send.at[at], sib_recv.at[at], me.sibling)
        for at, (source, target) in enumerate(blocks(me.dp, 1 - core))
    ]
    takes = [
        remote(source, target, sib_send.at[at], sib_recv.at[at], me.sibling)
        for at, (source, target) in enumerate(blocks(other, 1 - core))
    ]
    tell = remote(mine_ref, theirs, sib_send.at[6], sib_recv.at[6], me.sibling)
    rows_in = [
        pltpu.make_async_copy(x_hbm, xrow, own_sem.at[6]),
        pltpu.make_async_copy(cot_hbm, grow, own_sem.at[6]),
    ]
    y, x = me.y, me.x
    far = me.turn(2)

    def piece_of(stage, y_at, x_at, which):
        span = pl.ds(*STAGES[stage][which])
        if stage == 0:
            return wa.at[chip_span(y_at, x_at), span]
        return wb.at[span, chip_span(y_at, x_at)]

    def over_x(stage, y_at, x_at, which, slot):
        piece = piece_of(stage, y_at, x_at, which)
        return remote(piece, piece, x_send.at[stage, slot], x_recv.at[stage, slot], me.across)

    def over_y(stage, by, y_at, x_at, which, slot):
        piece = piece_of(stage, y_at, x_at, which)
        way = 0 if by > 0 else 1
        return remote(piece, piece, y_send.at[stage, way, slot], y_recv.at[stage, way, slot], me.beside(by))

    sent = []

    def start(copy):
        copy.start()
        sent.append(copy)

    def own_first(stage):
        for which in (0, 1):
            start(over_x(stage, y, x, which, which))
        for which in (2, 3):
            for by in (1, -1):
                start(over_y(stage, by, y, x, which, which))

    def own_second(stage):
        for which in (2, 3):
            start(over_x(stage, y, x, which, which))
        for which in (0, 1):
            for by in (1, -1):
                start(over_y(stage, by, y, x, which, which))

    def pass_near(stage):
        for which in (2, 3):
            for by in (1, -1):
                source = me.turn(-by)
                over_y(stage, by, source, x, which, which).wait_recv()
                if (which == 2) == (by > 0):
                    start(over_y(stage, by, source, x, which, 6))
                start(over_x(stage, source, x, which, 2 * which + (0 if by > 0 else 1)))

    def pass_crossed(stage):
        for which in (0, 1):
            over_x(stage, y, 1 - x, which, which).wait_recv()
            for by in (1, -1):
                start(over_y(stage, by, y, 1 - x, which, 4 + which))

    def pass_far(stage):
        for which, by in ((2, 1), (3, -1)):
            over_y(stage, by, far, x, which, 6).wait_recv()
            start(over_x(stage, far, x, which, 6 + which))

    def pass_on(stage):
        for which, by in ((0, 1), (1, -1)):
            source = me.turn(-by)
            over_y(stage, by, source, x, which, which).wait_recv()
            start(over_y(stage, by, source, x, which, 7))

    def pass_on_crossed(stage):
        for which, by in ((0, 1), (1, -1)):
            source = me.turn(-by)
            over_y(stage, by, source, 1 - x, which, 4 + which).wait_recv()
            start(over_y(stage, by, source, 1 - x, which, 8))

    def settle(stage):
        for which, by in ((0, -1), (1, 1)):
            source = me.turn(-by)
            over_y(stage, by, source, x, which, which).wait_recv()
            over_y(stage, by, source, 1 - x, which, 4 + which).wait_recv()
        for which in (2, 3):
            over_x(stage, y, 1 - x, which, which).wait_recv()
            for by in (1, -1):
                over_x(stage, me.turn(-by), 1 - x, which, 2 * which + (0 if by > 0 else 1)).wait_recv()
            over_x(stage, far, 1 - x, which, 6 + which).wait_recv()
        for which, by in ((0, 1), (1, -1)):
            over_y(stage, by, far, x, which, 7).wait_recv()
            over_y(stage, by, far, 1 - x, which, 8).wait_recv()

    def band(at):
        return pl.ds(pl.multiple_of(at * ROWS, ROWS), ROWS)

    def slot(i):
        return pl.ds(pl.multiple_of(i * SLOT, SLOT), SLOT)

    def slot_band(i, at):
        return pl.ds(pl.multiple_of(i * SLOT + at * ROWS, ROWS), ROWS)

    def standard(rows):
        average = jnp.mean(rows, axis=-1, keepdims=True)
        centred = rows - average
        variance = jnp.mean(centred * centred, axis=-1, keepdims=True)
        scale = lax.rsqrt(variance + EPSILON)
        return centred * scale, scale

    def spread_buffer(back):
        return grads if back else normed

    def to_z(back, m, i, k):
        piece = spread_buffer(back).at[slot_band(i, z)]
        return remote(piece, piece, agz_s.at[back, m, k], agz_r.at[back, m, k], me.z_peer(1 + k))

    def from_z(back, m, i, k):
        piece = spread_buffer(back).at[slot_band(i, lax.rem(z + 3 - k, 4))]
        return remote(piece, piece, agz_s.at[back, m, k], agz_r.at[back, m, k], me.z_peer(3 - k))

    def to_sibling(back, m, i, k):
        piece = spread_buffer(back).at[slot_band(i, lax.rem(z + 3 - k, 4))]
        return remote(piece, piece, ags_s.at[back, m, k], ags_r.at[back, m, k], me.sibling)

    def spread_own(back, m):
        i = 2 * m + core
        if back:
            grads[slot_band(i, z)] = grow[m]
        else:
            xhat, _ = standard(xrow[m].astype(F32))
            normed[slot_band(i, z)] = (xhat * gain_ref[...] + shift_ref[...]).astype(BF)
        for k in range(3):
            to_z(back, m, i, k).start()
        to_sibling(back, m, i, 3).start()

    def relay(back, i):
        m = i // 2
        for k in range(3):
            from_z(back, m, i, k).wait_recv()
            to_sibling(back, m, i, k).start()

    def await_rows(back, i):
        m = i // 2

        @pl.when(lax.rem(i, 2) != core)
        def _():
            for k in range(4):
                to_sibling(back, m, i, k).wait_recv()

    def part_at(i):
        return (1 - lax.rem(i + core, 2)) * (i // 2) + lax.rem(i + core, 2) * (2 + i // 2)

    def to_pair(back, i):
        m = i // 2
        return remote(part.at[2 + m], got.at[m], par_s.at[back, m], par_r.at[back, m], me.sibling)

    def sum_to_z(back, m, k):
        peer = me.z_peer(1 + k)
        return remote(
            part.at[m, band(peer["tensor"])],
            zgot.at[back * 2 + m, k],
            rsz_s.at[back, m, k],
            rsz_r.at[back, m, k],
            peer,
        )

    def pair_add(back, m):
        to_pair(back, 2 * m + core).wait_recv()
        part[m] = (part[m].astype(F32) + got[m].astype(F32)).astype(BF)
        if back == 0:
            pl.semaphore_signal(pair_free.at[m], inc=1, device_id=me.sibling, device_id_type=MESH)

    def pair_spread(back, m):
        for k in range(3):
            sum_to_z(back, m, k).start()

    def pair_sum(back, m):
        pair_add(back, m)
        pair_spread(back, m)

    def pair_sent(back, m):
        for k in range(3):
            sum_to_z(back, m, k).wait_send()

    def aside(m):
        return pltpu.make_async_copy(part.at[m], aside_out.at[m], aside_s.at[0, m])

    def back_again(m):
        return pltpu.make_async_copy(aside_out.at[m], part.at[m], aside_s.at[1, m])

    def row_sum(back, m):
        total = part[m, band(z)].astype(F32)
        for k in range(3):
            sum_to_z(back, m, k).wait_recv()
            total = total + zgot[back * 2 + m, k].astype(F32)
        return total

    def onward(back, m):
        target = grow if back else xrow
        return remote(zgot.at[back * 2 + m, 0], target.at[m], sec_s.at[back, m], sec_r.at[back, m], {"section": 1 - back})

    def keep(back, m):
        target = ig_out if back else lo_out
        return pltpu.make_async_copy(zgot.at[back * 2 + m, 0], target.at[m], keep_s.at[back, m])

    def finish_forward(m):
        zgot[m, 0] = (xrow[m].astype(F32) + row_sum(0, m) + (ob_ref[...] + db_ref[...])).astype(BF)
        keep(0, m).start()

        @pl.when(section == 0)
        def _():
            onward(0, m).start()

    def finish_backward(m):
        grad = row_sum(1, m)
        xhat, scale = standard(xrow[m].astype(F32))
        above = grow[m].astype(F32)
        tally[0, 0:1, :] += jnp.sum(grad * xhat, axis=0, keepdims=True)
        tally[0, 1:2, :] += jnp.sum(grad, axis=0, keepdims=True)
        tally[0, 2:3, :] += jnp.sum(above, axis=0, keepdims=True)
        a = grad * gain_ref[...]
        inner = a - jnp.mean(a, axis=-1, keepdims=True) - xhat * jnp.mean(a * xhat, axis=-1, keepdims=True)
        zgot[2 + m, 0] = (above + inner * scale).astype(BF)
        keep(1, m).start()

        @pl.when(section == 1)
        def _():
            onward(1, m).start()

    lanes = lax.broadcasted_iota(jnp.int32, (SLOT, 128), 1) % HD
    early = lanes < ROT // 2

    places = lax.broadcasted_iota(jnp.int32, (SLOT, 128), 0)

    def tables(i):
        first = places < split[pl.ds(i, 1), :]
        cosine, sine = cos_ref[...], sin_ref[...]
        cos_at, sin_at = ctab[pl.ds(i, 1), :], stab[pl.ds(i, 1), :]
        return (
            jnp.where(first, cosine, cosine * cos_at + sine * sin_at),
            jnp.where(first, sine, sine * cos_at - cosine * sin_at) * jnp.where(early, -1.0, 1.0),
        )

    def turned(values, table, sign):
        halves = []
        for at in (0, 128):
            piece = values[:, at : at + 128]
            swapped = jnp.where(early, pltpu.roll(piece, 128 - ROT // 2, 1), pltpu.roll(piece, ROT // 2, 1))
            halves.append(piece * table[0] + swapped * (table[1] * sign))
        return jnp.concatenate(halves, axis=1)

    def head_mask(head):
        lane = lax.broadcasted_iota(jnp.int32, (1, MIX), 1)
        return jnp.where(lane // HD == head, 1.0, 0.0).astype(BF)

    def forward_first(i):
        rows = normed[slot(i)]
        projected = dot(rows, wa[:, 0:QKV]) + bias[0:1, 0:QKV]
        table = tables(i)
        queries = turned(projected[:, 0:MIX], table, 1.0).astype(BF)
        keys = turned(projected[:, MIX : 2 * MIX], table, 1.0).astype(BF)
        values = projected[:, 2 * MIX : 3 * MIX].astype(BF)
        qkv[slot(i), 0:MIX] = queries
        qkv[slot(i), MIX : 2 * MIX] = keys
        qkv[slot(i), 2 * MIX : 3 * MIX] = values
        at = split[pl.ds(i, 1), :]
        at = jnp.concatenate([at, at], axis=1)
        row_at = lax.broadcasted_iota(jnp.int32, (SLOT, SLOT), 0)
        key_at = lax.broadcasted_iota(jnp.int32, (SLOT, SLOT), 1)
        same = jnp.where(row_at < at, 1, 0) == jnp.where(key_at < at, 1, 0)
        allowed = (key_at <= row_at) & same
        mixed = jnp.zeros((SLOT, MIX), F32)
        for head in range(4):
            mask = head_mask(head)
            scores = jnp.where(allowed, dot_nt(queries * mask, keys) * HD**-0.5, -1e30)
            weights = jnp.exp(scores - jnp.max(scores, axis=-1, keepdims=True))
            chances = (weights / jnp.sum(weights, axis=-1, keepdims=True)).astype(BF)
            probs[i, head] = chances
            mixed = mixed + dot(chances, values * mask)
        hcat[slot(i), 0:MIX] = mixed.astype(BF)
        v = dot(rows, wa[:, QKV:A_COLS]) + bias[0:1, QKV:A_COLS]
        root = np.sqrt(2 / np.pi).astype(np.float32)
        square = v * v
        bent = jnp.tanh(root * (v + 0.044715 * (square * v)))
        half = 0.5 * (1.0 + bent)
        hcat[slot(i), MIX:B_COLS] = (v * half).astype(BF)
        slope[slot(i)] = (half + 0.5 * v * (1.0 - bent * bent) * (root * (1.0 + 3 * 0.044715 * square))).astype(BF)

    def forward_second(i):
        for at in (0, D // 2):
            span = slice(at, at + D // 2)
            part[part_at(i), :, span] = dot(hcat[slot(i)], wb[:, span]).astype(BF)

    def backward_first(i):
        grad_hidden = dot_nt(grads[slot(i)], wb[...])
        grad_pre = (grad_hidden[:, MIX:B_COLS] * slope[slot(i)].astype(F32)).astype(BF)
        gproj[slot(i), QKV:A_COLS] = grad_pre
        sum_a[0:1, QKV:A_COLS] += jnp.sum(grad_pre.astype(F32), axis=0, keepdims=True)
        grad_mixed = grad_hidden[:, 0:MIX].astype(BF)
        queries = qkv[slot(i), 0:MIX]
        keys = qkv[slot(i), MIX : 2 * MIX]
        values = qkv[slot(i), 2 * MIX : 3 * MIX]
        zero = jnp.zeros((SLOT, MIX), F32)
        grad_queries, grad_keys, grad_values = zero, zero, zero
        for head in range(4):
            mask = head_mask(head)
            chances = probs[i, head]
            masked = grad_mixed * mask
            grad_values = grad_values + dot_tn(chances, masked)
            grad_probs = dot_nt(masked, values)
            wide = chances.astype(F32)
            centre = jnp.sum(wide * grad_probs, axis=-1, keepdims=True)
            grad_scores = (wide * (grad_probs - centre)).astype(BF)
            grad_queries = grad_queries + dot(grad_scores, keys * mask)
            grad_keys = grad_keys + dot_tn(grad_scores, queries * mask)
        table = tables(i)
        pieces = (
            turned(grad_queries * HD**-0.5, table, -1.0).astype(BF),
            turned(grad_keys * HD**-0.5, table, -1.0).astype(BF),
            grad_values.astype(BF),
        )
        for at, piece in enumerate(pieces):
            span = slice(at * MIX, (at + 1) * MIX)
            gproj[slot(i), span] = piece
            sum_a[0:1, span] += jnp.sum(piece.astype(F32), axis=0, keepdims=True)

    def backward_second(i):
        for at in (0, D // 2):
            span = slice(at, at + D // 2)
            part[part_at(i), :, span] = dot_nt(gproj[slot(i)], wa[span, :]).astype(BF)

    for copy in holds + gives:
        copy.start()
    tell.start()

    @pl.when(section == 0)
    def _():
        rows_in[0].start()

    @pl.when(section == 1)
    def _():
        rows_in[1].start()

    sum_a[...] = jnp.zeros_like(sum_a)
    tally[0] = jnp.zeros((8, D), F32)
    for at in range(4):
        holds[at].wait()
        takes[at].wait_recv()
    own_first(0)
    own_second(0)

    @pl.when(section == 0)
    def _():
        rows_in[0].wait()
        for m in range(2):
            spread_own(0, m)

    @pl.when(section == 1)
    def _():
        rows_in[1].wait()
        for m in range(2):
            spread_own(1, m)

    for at in (4, 5):
        holds[at].wait()
        takes[at].wait_recv()
    for at in range(3):
        bias[0:1, at * MIX : (at + 1) * MIX] = jnp.where(
            core == 0, qb_ref[at : at + 1, 0:MIX], qb_ref[at : at + 1, MIX : 2 * MIX]
        )
    bias[0:1, QKV:A_COLS] = jnp.where(core == 0, ub_ref[0:1, 0:UP], ub_ref[0:1, UP : 2 * UP])
    tell.wait_recv()
    for i in range(4):
        at = jnp.where(core == i % 2, mine_ref[i // 2 : i // 2 + 1, :], theirs[i // 2 : i // 2 + 1, :])
        split[i : i + 1, :] = at
        here = places == at
        ctab[i : i + 1, :] = jnp.sum(jnp.where(here, cos_ref[...], 0.0), axis=0, keepdims=True)
        stab[i : i + 1, :] = jnp.sum(jnp.where(here, sin_ref[...], 0.0), axis=0, keepdims=True)

    pass_near(0)
    pass_crossed(0)

    def relay_early(m):
        @pl.when(section == 0)
        def _():
            relay(0, 2 * m + core)

        @pl.when(section == 1)
        def _():
            relay(1, 2 * m + core)

    relay_early(0)
    pass_on(0)
    own_first(1)
    pass_far(0)
    relay_early(1)
    pass_on_crossed(0)
    own_second(1)
    settle(0)
    pass_near(1)

    def forward_early(i):
        @pl.when(section == 0)
        def _():
            await_rows(0, i)
            forward_first(i)

    forward_early(0)
    pass_crossed(1)
    forward_early(1)
    pass_on(1)
    pass_far(1)
    forward_early(2)
    forward_early(3)
    pass_on_crossed(1)
    settle(1)

    def forward_last(i):
        forward_second(i)

        @pl.when(lax.rem(i, 2) != core)
        def _():
            to_pair(0, i).start()

    def finish_forward_all():
        for m in range(2):
            finish_forward(m)

    @pl.when(section == 0)
    def _():
        def step(i, _):
            forward_last(i)

            @pl.when(i == 1 + core)
            def _():
                pair_sum(0, 0)

            return 0

        lax.fori_loop(0, 4, step, 0)
        pair_sum(0, 1)
        finish_forward_all()

        @pl.when(core == 0)
        def _():
            onward(1, 0).wait_recv()
            spread_own(1, 0)
            relay(1, 0)

    @pl.when(section == 1)
    def _():
        def arrive(m):
            onward(0, m).wait_recv()
            spread_own(0, m)

        arrive(0)

        @pl.when(core == 0)
        def _():
            relay(0, 0)

        def step(i, _):
            await_rows(0, i)
            forward_first(i)

            @pl.when((i == 0) & (core == 0))
            def _():
                arrive(1)

            @pl.when((i < 3) & (lax.rem(i, 2) != core))
            def _():
                relay(0, i + 1)

            @pl.when((i > 0) & (lax.rem(i, 2) != core))
            def _():
                pair_add(0, (i - 1) // 2)
                aside((i - 1) // 2).start()

            forward_last(i)

            @pl.when((i == 0) & (core == 1))
            def _():
                arrive(1)

            return 0

        lax.fori_loop(0, 4, step, 0)

    def turn_of(k):
        return lax.rem(y + 2 - k + 4, 4)

    a_cuts = ((0, A_HALF), (A_HALF, A_COLS))
    b_cuts = ((0, B_HALF), (B_HALF, B_COLS))

    def term_a(y_at, x_at, half):
        lo, hi = a_cuts[half]
        return dot_tn(normed[:, chip_span(y_at, x_at)], gproj[:, lo:hi])

    def term_b(y_at, x_at, half):
        lo, hi = b_cuts[half]
        return dot_tn(hcat[:, lo:hi], grads[:, chip_span(y_at, x_at)])

    def cross(k):
        span = pl.ds(pl.multiple_of(k * MIX, MIX), MIX)
        there = pl.ds(pl.multiple_of((4 + k) * 256, 256), 256)
        return (
            remote(probs.at[k, 0], wb.at[pl.ds(0, MIX), there], xs.at[k, 0], xr.at[k, 0], me.across),
            remote(slope.at[:, span], wb.at[pl.ds(MIX, UP), there], xs.at[k, 1], xr.at[k, 1], me.across),
        )

    def cross_all():
        pl.semaphore_wait(free_sem, 1)

        def step(k, _):
            span = pl.ds(pl.multiple_of(k * MIX, MIX), MIX)
            total = term_b(turn_of(k), 1 - x, 0).astype(BF)
            probs[k, 0] = total[0:MIX]
            slope[0 : B_HALF - MIX, span] = total[MIX:B_HALF]
            slope[B_HALF - MIX : UP, span] = term_b(turn_of(k), 1 - x, 1).astype(BF)
            for copy in cross(k):
                copy.start()
            return 0

        lax.fori_loop(0, 4, step, 0)

    def crossed(k):
        for copy in cross(k):
            copy.wait_recv()

    def from_across(k, half):
        lo, hi = b_cuts[half]
        return wb[lo:hi, (4 + k) * 256 : (5 + k) * 256].astype(F32)

    def a_place(at):
        return wa.at[pl.ds(pl.multiple_of(at * 256, 256), 256)]

    def b_place(at):
        return wb.at[:, pl.ds(at * 256, 256)]

    a_spans = (pl.ds(0, A_HALF), pl.ds(A_HALF, A_HALF))
    b_spans = (pl.ds(0, B_HALF), pl.ds(B_HALF, B_HALF))

    def far_piece(way, x_at):
        source = wa.at[pl.ds(pl.multiple_of(x_at * 256, 256), 256), a_spans[way]]
        return remote(source, half_a.at[way, x_at], fs.at[way, x_at], fr.at[way, x_at], me.beside(1 - 2 * way))

    def far_piece_b(way):
        source = wb.at[b_spans[way], pl.ds(0, 256)]
        return remote(source, half_b.at[way], fs.at[way, 2], fr.at[way, 2], me.beside(1 - 2 * way))

    def near_piece(way, x_at):
        source = a_place(2 + 2 * way + x_at)
        return remote(source, got_a.at[way, x_at], ns.at[way, x_at], nr.at[way, x_at], me.beside(1 - 2 * way))

    def near_piece_b(way):
        return remote(b_place(1 + way), got_b.at[way], ns.at[way, 2], nr.at[way, 2], me.beside(1 - 2 * way))

    def cross_last():
        return remote(a_place(6), xa_in, xs.at[4, 0], xr.at[4, 0], me.across)

    def send_far(x_at):
        target = pl.ds(pl.multiple_of(x_at * 256, 256), 256)
        for way, (lo, hi) in enumerate(a_cuts):
            wa[target, lo:hi] = term_a(far, x_at, way).astype(BF)
            start(far_piece(way, x_at))

    def send_near(way, x_at):
        target = pl.ds(pl.multiple_of((2 + 2 * way + x_at) * 256, 256), 256)
        for half in (1 - way, way):
            lo, hi = a_cuts[half]
            total = term_a(me.turn(1 - 2 * way), x_at, half)
            if half == way:
                far_piece(way, x_at).wait_recv()
                total = total + half_a[way, x_at].astype(F32)
            wa[target, lo:hi] = total.astype(BF)
        start(near_piece(way, x_at))

    def send_far_b():
        crossed(0)
        for way, (lo, hi) in enumerate(b_cuts):
            wb[lo:hi, 0:256] = (term_b(far, x, way) + from_across(0, way)).astype(BF)
            start(far_piece_b(way))

    def send_near_b(way):
        crossed(1 + 2 * way)
        span = slice((1 + way) * 256, (2 + way) * 256)
        for half in (1 - way, way):
            lo, hi = b_cuts[half]
            total = term_b(me.turn(1 - 2 * way), x, half) + from_across(1 + 2 * way, half)
            if half == way:
                far_piece_b(way).wait_recv()
                total = total + half_b[way].astype(F32)
            wb[lo:hi, span] = total.astype(BF)
        start(near_piece_b(way))

    def arrived_a(x_at, at):
        for half, (lo, hi) in enumerate(a_cuts):
            total = term_a(y, x_at, half)
            for way in (0, 1):
                if half == 0:
                    near_piece(way, x_at).wait_recv()
                total = total + got_a[way, x_at, :, lo:hi].astype(F32)
            wa[at * 256 : (at + 1) * 256, lo:hi] = total.astype(BF)

    def arrived_b(at):
        crossed(2)
        for half, (lo, hi) in enumerate(b_cuts):
            total = term_b(y, x, half) + from_across(2, half)
            for way in (0, 1):
                if half == 0:
                    near_piece_b(way).wait_recv()
                total = total + got_b[way, lo:hi].astype(F32)
            wb[lo:hi, at * 256 : (at + 1) * 256] = total.astype(BF)

    near_z = {"tensor": z + 1 - 2 * lax.rem(z, 2)}
    near_y = {"dp": me.at(y + 1 - 2 * lax.rem(y, 2), x, core)}
    partners = (me.across, near_y, me.beside(2), near_z, me.z_peer(2), me.sibling)

    def exchange(step):
        return remote(tally.at[step], came.at[step], ts.at[step], tr.at[step], partners[step])

    def fold(step):
        exchange(step).wait_recv()
        total = tally[step] + came[step]
        if step < 3:
            tally[step + 1] = total
        else:
            tally[step + 1, 0:3] = total[0:3]
            tally[step + 1, 3:8] = tally[step, 3:8]
        if step < 5:
            start(exchange(step + 1))

    for copy in sent:
        copy.wait_send()
    sent.clear()

    def backward_step(i, _):
        own = lax.rem(i, 2) == core

        @pl.when((section == 0) & (i < 3) & jnp.logical_not(own))
        def _():
            onward(1, (i + 1) // 2).wait_recv()
            spread_own(1, (i + 1) // 2)

        await_rows(1, i)
        backward_first(i)

        @pl.when((section == 0) & (i < 3) & jnp.logical_not(own))
        def _():
            relay(1, i + 1)

        @pl.when(i == 3)
        def _():
            pl.semaphore_signal(free_sem, inc=1, device_id=me.across, device_id_type=MESH)

        @pl.when((section == 0) & (i == 3))
        def _():
            cross_all()

        @pl.when((i >= 1) & jnp.logical_not(own))
        def _():
            pair_sum(1, (i - 1) // 2)

        @pl.when((i >= 2) & own)
        def _():
            finish_backward(0)

        @pl.when((section == 1) & (core == 1) & (i == 0))
        def _():
            pair_add(0, 1)
            aside(1).start()

        @pl.when((section == 0) & own)
        def _():
            pair_sent(0, i // 2)

        @pl.when((section == 1) & own)
        def _():
            aside(i // 2).wait()

        @pl.when(jnp.logical_not(own))
        def _():
            to_pair(0, i).wait_send()

        backward_second(i)

        @pl.when(jnp.logical_not(own))
        def _():
            pl.semaphore_wait(pair_free.at[i // 2], 1)
            to_pair(1, i).start()

        return 0

    lax.fori_loop(0, 4, backward_step, 0)

    @pl.when(section == 1)
    def _():
        @pl.when(core == 1)
        def _():
            pair_sum(1, 1)

        finish_backward(1)
        cross_all()

    send_far(1 - x)
    send_far(x)

    @pl.when((section == 0) & (core == 1))
    def _():
        pair_sum(1, 1)

    @pl.when(section == 1)
    def _():
        for m in range(2):
            pair_sent(1, m)
            back_again(m).start()

    send_far_b()

    @pl.when(section == 1)
    def _():
        for m in range(2):
            back_again(m).wait()
            pair_spread(0, m)

    for way in (0, 1):
        send_near(way, 1 - x)

    @pl.when(section == 0)
    def _():
        finish_backward(1)

    tally[0, 3:4, 0:A_COLS] = sum_a[0:1]
    start(exchange(0))
    for way in (0, 1):
        send_near(way, x)
    fold(0)
    for way in (0, 1):
        send_near_b(way)
    fold(1)

    @pl.when(section == 1)
    def _():
        finish_forward_all()

    arrived_a(1 - x, 6)
    start(cross_last())
    fold(2)
    arrived_b(3)
    fold(3)

    def result(half, peer, at):
        rows = pl.ds(pl.multiple_of(7 * 256 + half * 128, 128), 128)
        cols = pl.ds(pl.multiple_of(3 * 256 + half * 128, 128), 128)
        sources = [wa.at[rows, pl.ds(k * MIX, MIX)] for k in range(3)]
        sources += [wa.at[rows, pl.ds(QKV, UP)], wb.at[pl.ds(0, MIX), cols], wb.at[pl.ds(MIX, UP), cols]]
        targets = [gq_out.at[k, :, place(at, MIX)] for k in range(3)]
        targets += [gu_out.at[:, place(at, UP)], go_out.at[place(at, MIX), :], gd_out.at[place(at, UP), :]]
        if peer:
            return [
                remote(source, target, end_s.at[k], end_r.at[k], me.sibling)
                for k, (source, target) in enumerate(zip(sources, targets))
            ]
        return [
            pltpu.make_async_copy(source, target, end_k.at[k])
            for k, (source, target) in enumerate(zip(sources, targets))
        ]

    outgoing, staying = result(1 - core, True, core), result(core, False, core)
    incoming = result(1 - core, True, 1 - core)
    for at in (4, 5):
        outgoing[at].start()
        staying[at].start()
    fold(4)
    arrived_a(x, 7)
    fold(5)
    sums_ref[...] = tally[6]
    for at in range(3):
        span = slice(at * MIX, (at + 1) * MIX)
        ours, others = tally[6, 3:4, span], came[5, 3:4, span]
        gqb_ref[at : at + 1, 0:MIX] = jnp.where(core == 0, ours, others)
        gqb_ref[at : at + 1, MIX : 2 * MIX] = jnp.where(core == 0, others, ours)
    ours, others = tally[6, 3:4, QKV:A_COLS], came[5, 3:4, QKV:A_COLS]
    gub_ref[0:1, 0:UP] = jnp.where(core == 0, ours, others)
    gub_ref[0:1, UP : 2 * UP] = jnp.where(core == 0, others, ours)
    cross_last().wait_recv()
    wa[7 * 256 : 8 * 256] = (wa[7 * 256 : 8 * 256].astype(F32) + xa_in[...].astype(F32)).astype(BF)
    for at in range(4):
        outgoing[at].start()
        staying[at].start()

    for copy in sent + gives + [tell]:
        copy.wait_send()
    for k in range(4):
        for copy in cross(k):
            copy.wait_send()
    for back in range(2):
        for m in range(2):
            mine = 2 * m + core
            for k in range(3):
                to_z(back, m, mine, k).wait_send()
            for k in range(4):
                to_sibling(back, m, mine, k).wait_send()
            keep(back, m).wait()

        @pl.when(section == back)
        def _():
            for m in range(2):
                onward(back, m).wait_send()

        @pl.when(section != back)
        def _():
            for m in range(2):
                pair_sent(back, m)

    for m in range(2):
        to_pair(1, 2 * m + 1 - core).wait_send()
    for at in range(6):
        staying[at].wait()
        outgoing[at].wait_send()
        incoming[at].wait_recv()


def both_layers(rows_in, cotangent, qkv_w, up_w, out_w, down_w, bias_qkv, bias_up, bias_out, bias_down, gain, shift, mine):
    places = np.arange(SLOT, dtype=np.float32)
    frequency = (10000.0 ** (-(np.arange(ROT // 2, dtype=np.float32) * np.float32(2.0 / ROT)))).astype(np.float32)
    angles = (places[:, None] * frequency[None, :]).astype(np.float32).astype(np.float64)
    cosine = np.ones((SLOT, HD), np.float32)
    sine = np.zeros((SLOT, HD), np.float32)
    cosine[:, 0:ROT] = np.tile(np.cos(angles), (1, 2))
    sine[:, 0:ROT] = np.tile(np.sin(angles), (1, 2))
    cosine, sine = (jnp.asarray(np.tile(table, (1, 2))) for table in (cosine, sine))
    any_ = pl.BlockSpec(memory_space=pl.ANY)
    vmem = pl.BlockSpec(memory_space=pltpu.VMEM)
    dma = pltpu.SemaphoreType.DMA
    shape = jax.ShapeDtypeStruct
    return pl.pallas_call(
        layers_kernel,
        out_shape=(
            shape((2, ROWS, D), BF),
            shape((2, ROWS, D), BF),
            shape((3, 128, 2 * MIX), BF),
            shape((128, 2 * UP), BF),
            shape((2 * MIX, 128), BF),
            shape((2 * UP, 128), BF),
            shape((8, D), F32),
            shape((3, 2 * MIX), F32),
            shape((1, 2 * UP), F32),
            shape((2, SLOT, D), BF),
        ),
        in_specs=[any_] * 6 + [vmem] * 9,
        out_specs=[any_] * 6 + [vmem] * 3 + [any_],
        scratch_shapes=[
            pltpu.VMEM((D, A_COLS), BF),
            pltpu.VMEM((B_COLS, D), BF),
            pltpu.VMEM((ALL, D), BF),
            pltpu.VMEM((ALL, D), BF),
            pltpu.VMEM((ALL, QKV), BF),
            pltpu.VMEM((ALL, B_COLS), BF),
            pltpu.VMEM((ALL, UP), BF),
            pltpu.VMEM((4, 4, SLOT, SLOT), BF),
            pltpu.VMEM((ALL, A_COLS), BF),
            pltpu.VMEM((4, SLOT, D), BF),
            pltpu.VMEM((2, SLOT, D), BF),
            pltpu.VMEM((4, 3, ROWS, D), BF),
            pltpu.VMEM((2, ROWS, D), BF),
            pltpu.VMEM((2, ROWS, D), BF),
            pltpu.VMEM((8, 128), F32),
            pltpu.VMEM((8, 128), F32),
            pltpu.VMEM((8, 128), jnp.int32),
            pltpu.VMEM((8, 128), jnp.int32),
            pltpu.VMEM((8, A_COLS), F32),
            pltpu.VMEM((2, 2, 256, A_HALF), BF),
            pltpu.VMEM((2, B_HALF, 256), BF),
            pltpu.VMEM((2, 2, 256, A_COLS), BF),
            pltpu.VMEM((2, B_COLS, 256), BF),
            pltpu.VMEM((256, A_COLS), BF),
            pltpu.VMEM((8, A_COLS), F32),
            pltpu.VMEM((7, 8, D), F32),
            pltpu.VMEM((6, 8, D), F32),
            dma((7,)),
            dma((2, 10)),
            dma((2, 10)),
            dma((2, 2, 9)),
            dma((2, 2, 9)),
            dma((7,)),
            dma((7,)),
            dma((2, 2, 3)),
            dma((2, 2, 3)),
            dma((2, 2, 4)),
            dma((2, 2, 4)),
            dma((2, 2)),
            dma((2, 2)),
            dma((2, 2, 3)),
            dma((2, 2, 3)),
            dma((2, 2)),
            dma((2, 2)),
            dma((5, 2)),
            dma((5, 2)),
            dma((2, 3)),
            dma((2, 3)),
            dma((2, 3)),
            dma((2, 3)),
            dma((6,)),
            dma((6,)),
            dma((6,)),
            dma((6,)),
            dma((6,)),
            dma((2, 2)),
            pltpu.SemaphoreType.REGULAR,
            pltpu.SemaphoreType.REGULAR((2,)),
            dma((2, 2)),
        ],
        compiler_params=pltpu.CompilerParams(
            collective_id=1, has_side_effects=True, vmem_limit_bytes=VMEM_LIMIT
        ),
        name="both_layers",
    )(
        rows_in, cotangent, qkv_w, up_w, out_w, down_w,
        bias_qkv, bias_up, bias_out, bias_down, gain, shift, mine, cosine, sine,
    )


def shards(
    inputs,
    cotangent,
    doc_split,
    qkv_weight,
    qkv_bias,
    out_weight,
    out_bias,
    fc1_weight,
    fc1_bias,
    fc2_weight,
    fc2_bias,
    ln_gain,
    ln_bias,
):
    mine = jnp.broadcast_to(doc_split[None], (4, 2, 128)).reshape(8, 128)
    layer_out, input_grad, grad_qkv, grad_up, grad_out, grad_down, sums, grad_qkv_bias, grad_up_bias, _ = both_layers(
        inputs[:, 0],
        cotangent[:, 0],
        qkv_weight[0].transpose(1, 0, 2),
        fc1_weight[0],
        out_weight[0],
        fc2_weight[0],
        qkv_bias[0],
        fc1_bias,
        out_bias,
        fc2_bias,
        ln_gain,
        ln_bias,
        mine,
    )
    return (
        layer_out[None, :, None],
        input_grad[None, :, None],
        grad_qkv.transpose(1, 0, 2).astype(F32)[None],
        grad_qkv_bias[None],
        grad_out.astype(F32)[None],
        sums[2:3],
        grad_up.astype(F32)[None],
        grad_up_bias,
        grad_down.astype(F32)[None],
        sums[2:3],
        sums[0:1],
        sums[1:2],
    )


def solution(mesh):
    rows = P(None, "dp", "tensor", None)
    placed_weights = (
        P("section", "dp", None, "tensor"),
        P("section", None, "tensor"),
        P("section", "tensor", "dp"),
        P("section", None),
        P("section", "dp", "tensor"),
        P("section", "tensor"),
        P("section", "tensor", "dp"),
        P("section", None),
        P("section", None),
        P("section", None),
    )
    out_rows = P("section", None, "dp", "tensor", None)
    return jax.shard_map(
        shards,
        mesh=mesh,
        in_specs=(rows, rows, P(None, "dp")) + placed_weights,
        out_specs=(out_rows, out_rows) + placed_weights,
        check_vma=False,
    )
```

time: 386 us -> 360 us (0.933)
  the two profiles are of different devices: /device:TPU:3 before, /device:TPU:1 now
where the time goes in v3:
time: 360 us; the launch traced here: 354 us
  Pallas kernels  338 us (94%)
  local copies, waits for them, and re-layouts  8.42 us (2%)
  other arithmetic  6.87 us (2%)
    pallas_call x1, Pallas kernels, both_layers(): pl.pallas_call(layers_kernel, out_shape=(shape((2, ROWS, D), BF), shape((...  338 us

profile of v3, /device:TPU:1, one launch (start us, length us, event | category | flops | bytes accessed | tf_op | source)
XLA Modules:
  0.0 354.3 jit_solution(7813596979199976231)
XLA Ops:
  0.6 0.7 broadcast_in_dim.46
  1.3 0.1 broadcast_in_dim.47
  1.4 0.7 broadcast_in_dim.48.mine_ref
  2.1 1.3 copy.35
  3.3 338.1 %both_layers.1 = (bf16[2,64,2048]{2,1,0:T(8,128)(2,1)}, bf16[2,64,2048]{2,1,0:T(8,128)(2,1)}, bf16[3,128,512]{2,1,0:T(8,128)(2,1)}, bf16[128,2048]{1,0:T(8,128)(...) custom-call(bf16[2,64,2048]{2,1,0:T(8,128)(2,1)} %bitcast.34, ...), custom_call_target="tpu_custom_call" | custom-call | tf_op jit(solution)/shard_map/both_layers/pallas_call | solution.py:968
  341.4 0.0 copy-start
  341.4 1.4 copy.32
  342.8 1.6 fusion
  344.4 0.0 copy-start.3
  344.4 1.6 bitcast_convert_fusion.2
  346.0 0.0 copy-start.2
  346.0 2.0 convert_bitcast_fusion
  348.0 0.0 copy-start.1
  348.0 2.2 bitcast_convert_fusion.1
  350.2 0.0 copy-done
  350.2 1.0 bitcast_convert_fusion
  351.2 0.0 copy-done.3
  351.2 0.6 copy.40
  351.8 0.0 copy-done.2
  351.8 0.8 copy.41
  352.6 0.0 copy-done.1
  352.6 0.8 copy.42
  353.4 0.0 copy-done.4
  353.4 0.6 copy.43
  (1 shorter events, 0.0 us)
Async XLA Ops:
  341.4 8.8 %copy-start = (bf16[2048,128]{1,0:T(8,128)(2,1)S(1)}, bf16[2048,128]{1,0:T(8,128)(2,1)}, u32[]{:S(2)}) copy-start(bf16[2048,128]{1,0:T(8,128)(2,1)} %get-tuple-element.29) | copy-start | bytes 1572868
  344.4 6.9 %copy-start.3 = (f32[1,2048]{1,0:T(1,128)}, f32[1,2048]{1,0:T(1,128)S(1)}, u32[]{:S(2)}) copy-start(f32[1,2048]{1,0:T(1,128)S(1)} %get-tuple-element.98) | copy-start | bytes 24580
  346.0 5.9 %copy-start.2 = (bf16[2,64,2048]{2,1,0:T(8,128)(2,1)S(1)}, bf16[2,64,2048]{2,1,0:T(8,128)(2,1)}, u32[]{:S(2)}) copy-start(bf16[2,64,2048]{2,1,0:T(8,128)(2,1)} %get-tuple-element.21) | copy-start | bytes 1572868
  348.0 4.6 %copy-start.1 = (bf16[2,64,2048]{2,1,0:T(8,128)(2,1)S(1)}, bf16[2,64,2048]{2,1,0:T(8,128)(2,1)}, u32[]{:S(2)}) copy-start(bf16[2,64,2048]{2,1,0:T(8,128)(2,1)} %get-tuple-element.22) | copy-start | bytes 1572868
  350.2 3.2 copy-start.4

commit v4 on v3

--- a/solution.py
+++ b/solution.py
@@ -18,6 +18,7 @@
 D = 2048
 SLOT = 256
 ROWS = 64
+PART = ROWS // 2
 QKV = 768
 UP = 1024
 A_COLS = QKV + UP
@@ -88,7 +89,7 @@
     qb_ref, ub_ref, ob_ref, db_ref, gain_ref, shift_ref, mine_ref, cos_ref, sin_ref,
     lo_out, ig_out, gq_out, gu_out, go_out, gd_out, sums_ref, gqb_ref, gub_ref, aside_out,
     wa, wb, normed, grads, qkv, hcat, slope, probs, gproj, part, got, zgot, xrow, grow, ctab, stab, split, theirs, bias,
-    half_a, half_b, got_a, got_b, xa_in, sum_a, tally, came,
+    far_a, half_a, half_b, got_a, got_b, xa_in, sum_a, tally, came,
     own_sem, x_send, x_recv, y_send, y_recv, sib_send, sib_recv,
     agz_s, agz_r, ags_s, ags_r, par_s, par_r, rsz_s, rsz_r, sec_s, sec_r,
     xs, xr, fs, fr, ns, nr, ts, tr, end_s, end_r, end_k, keep_s, free_sem, pair_free, aside_s,
@@ -222,14 +223,16 @@
             over_y(stage, by, far, x, which, 7).wait_recv()
             over_y(stage, by, far, 1 - x, which, 8).wait_recv()
 
-    def band(at):
-        return pl.ds(pl.multiple_of(at * ROWS, ROWS), ROWS)
+    def band(at, h):
+        return pl.ds(pl.multiple_of(at * ROWS + h * PART, PART), PART)
 
     def slot(i):
         return pl.ds(pl.multiple_of(i * SLOT, SLOT), SLOT)
 
-    def slot_band(i, at):
-        return pl.ds(pl.multiple_of(i * SLOT + at * ROWS, ROWS), ROWS)
+    def slot_band(i, at, h):
+        return pl.ds(pl.multiple_of(i * SLOT + at * ROWS + h * PART, PART), PART)
+
+    halves = (slice(0, PART), slice(PART, ROWS))
 
     def standard(rows):
         average = jnp.mean(rows, axis=-1, keepdims=True)
@@ -241,77 +244,93 @@
     def spread_buffer(back):
         return grads if back else normed
 
-    def to_z(back, m, i, k):
-        piece = spread_buffer(back).at[slot_band(i, z)]
-        return remote(piece, piece, agz_s.at[back, m, k], agz_r.at[back, m, k], me.z_peer(1 + k))
-
-    def from_z(back, m, i, k):
-        piece = spread_buffer(back).at[slot_band(i, lax.rem(z + 3 - k, 4))]
-        return remote(piece, piece, agz_s.at[back, m, k], agz_r.at[back, m, k], me.z_peer(3 - k))
-
-    def to_sibling(back, m, i, k):
-        piece = spread_buffer(back).at[slot_band(i, lax.rem(z + 3 - k, 4))]
-        return remote(piece, piece, ags_s.at[back, m, k], ags_r.at[back, m, k], me.sibling)
-
-    def spread_own(back, m):
+    def to_z(back, m, i, k, h):
+        piece = spread_buffer(back).at[slot_band(i, z, h)]
+        at = 2 * k + h
+        return remote(piece, piece, agz_s.at[back, m, at], agz_r.at[back, m, at], me.z_peer(1 + k))
+
+    def from_z(back, m, i, k, h):
+        piece = spread_buffer(back).at[slot_band(i, lax.rem(z + 3 - k, 4), h)]
+        at = 2 * k + h
+        return remote(piece, piece, agz_s.at[back, m, at], agz_r.at[back, m, at], me.z_peer(3 - k))
+
+    def to_sibling(back, m, i, k, h):
+        piece = spread_buffer(back).at[slot_band(i, lax.rem(z + 3 - k, 4), h)]
+        at = 2 * k + h
+        return remote(piece, piece, ags_s.at[back, m, at], ags_r.at[back, m, at], me.sibling)
+
+    def spread_own(back, m, wait):
         i = 2 * m + core
-        if back:
-            grads[slot_band(i, z)] = grow[m]
-        else:
-            xhat, _ = standard(xrow[m].astype(F32))
-            normed[slot_band(i, z)] = (xhat * gain_ref[...] + shift_ref[...]).astype(BF)
-        for k in range(3):
-            to_z(back, m, i, k).start()
-        to_sibling(back, m, i, 3).start()
+        for h in range(2):
+            if wait:
+                onward(1 if back else 0, m, h).wait_recv()
+            if back:
+                grads[slot_band(i, z, h)] = grow[m, halves[h]]
+            else:
+                xhat, _ = standard(xrow[m, halves[h]].astype(F32))
+                normed[slot_band(i, z, h)] = (xhat * gain_ref[...] + shift_ref[...]).astype(BF)
+            for k in range(3):
+                to_z(back, m, i, k, h).start()
+            to_sibling(back, m, i, 3, h).start()
 
     def relay(back, i):
         m = i // 2
-        for k in range(3):
-            from_z(back, m, i, k).wait_recv()
-            to_sibling(back, m, i, k).start()
+        for h in range(2):
+            for k in range(3):
+                from_z(back, m, i, k, h).wait_recv()
+                to_sibling(back, m, i, k, h).start()
 
     def await_rows(back, i):
         m = i // 2
 
         @pl.when(lax.rem(i, 2) != core)
         def _():
-            for k in range(4):
-                to_sibling(back, m, i, k).wait_recv()
+            for h in range(2):
+                for k in range(4):
+                    to_sibling(back, m, i, k, h).wait_recv()
 
     def part_at(i):
         return (1 - lax.rem(i + core, 2)) * (i // 2) + lax.rem(i + core, 2) * (2 + i // 2)
 
-    def to_pair(back, i):
+    def to_pair(back, i, q):
         m = i // 2
-        return remote(part.at[2 + m], got.at[m], par_s.at[back, m], par_r.at[back, m], me.sibling)
-
-    def sum_to_z(back, m, k):
+        span = pl.ds(q * (D // 2), D // 2)
+        return remote(
+            part.at[2 + m, :, span], got.at[m, :, span], par_s.at[back, m, q], par_r.at[back, m, q], me.sibling
+        )
+
+    def sum_to_z(back, m, k, h):
         peer = me.z_peer(1 + k)
+        at = 2 * k + h
         return remote(
-            part.at[m, band(peer["tensor"])],
-            zgot.at[back * 2 + m, k],
-            rsz_s.at[back, m, k],
-            rsz_r.at[back, m, k],
+            part.at[m, band(peer["tensor"], h)],
+            zgot.at[back * 2 + m, k, pl.ds(h * PART, PART)],
+            rsz_s.at[back, m, at],
+            rsz_r.at[back, m, at],
             peer,
         )
 
     def pair_add(back, m):
-        to_pair(back, 2 * m + core).wait_recv()
-        part[m] = (part[m].astype(F32) + got[m].astype(F32)).astype(BF)
+        for q in range(2):
+            span = slice(q * (D // 2), (q + 1) * (D // 2))
+            to_pair(back, 2 * m + core, q).wait_recv()
+            part[m, :, span] = (part[m, :, span].astype(F32) + got[m, :, span].astype(F32)).astype(BF)
         if back == 0:
             pl.semaphore_signal(pair_free.at[m], inc=1, device_id=me.sibling, device_id_type=MESH)
 
     def pair_spread(back, m):
-        for k in range(3):
-            sum_to_z(back, m, k).start()
+        for h in range(2):
+            for k in range(3):
+                sum_to_z(back, m, k, h).start()
 
     def pair_sum(back, m):
         pair_add(back, m)
         pair_spread(back, m)
 
     def pair_sent(back, m):
-        for k in range(3):
-            sum_to_z(back, m, k).wait_send()
+        for h in range(2):
+            for k in range(3):
+                sum_to_z(back, m, k, h).wait_send()
 
     def aside(m):
         return pltpu.make_async_copy(part.at[m], aside_out.at[m], aside_s.at[0, m])
@@ -319,44 +338,57 @@
     def back_again(m):
         return pltpu.make_async_copy(aside_out.at[m], part.at[m], aside_s.at[1, m])
 
-    def row_sum(back, m):
-        total = part[m, band(z)].astype(F32)
+    def row_sum(back, m, h):
+        total = part[m, band(z, h)].astype(F32)
         for k in range(3):
-            sum_to_z(back, m, k).wait_recv()
-            total = total + zgot[back * 2 + m, k].astype(F32)
+            sum_to_z(back, m, k, h).wait_recv()
+            total = total + zgot[back * 2 + m, k, halves[h]].astype(F32)
         return total
 
-    def onward(back, m):
+    def onward(back, m, h):
         target = grow if back else xrow
-        return remote(zgot.at[back * 2 + m, 0], target.at[m], sec_s.at[back, m], sec_r.at[back, m], {"section": 1 - back})
+        span = pl.ds(h * PART, PART)
+        return remote(
+            zgot.at[back * 2 + m, 0, span],
+            target.at[m, span],
+            sec_s.at[back, m, h],
+            sec_r.at[back, m, h],
+            {"section": 1 - back},
+        )
 
     def keep(back, m):
         target = ig_out if back else lo_out
         return pltpu.make_async_copy(zgot.at[back * 2 + m, 0], target.at[m], keep_s.at[back, m])
 
     def finish_forward(m):
-        zgot[m, 0] = (xrow[m].astype(F32) + row_sum(0, m) + (ob_ref[...] + db_ref[...])).astype(BF)
+        for h in range(2):
+            total = row_sum(0, m, h) + (ob_ref[...] + db_ref[...])
+            zgot[m, 0, halves[h]] = (xrow[m, halves[h]].astype(F32) + total).astype(BF)
+
+            @pl.when(section == 0)
+            def _():
+                onward(0, m, h).start()
+
         keep(0, m).start()
 
-        @pl.when(section == 0)
-        def _():
-            onward(0, m).start()
-
     def finish_backward(m):
-        grad = row_sum(1, m)
-        xhat, scale = standard(xrow[m].astype(F32))
-        above = grow[m].astype(F32)
-        tally[0, 0:1, :] += jnp.sum(grad * xhat, axis=0, keepdims=True)
-        tally[0, 1:2, :] += jnp.sum(grad, axis=0, keepdims=True)
-        tally[0, 2:3, :] += jnp.sum(above, axis=0, keepdims=True)
-        a = grad * gain_ref[...]
-        inner = a - jnp.mean(a, axis=-1, keepdims=True) - xhat * jnp.mean(a * xhat, axis=-1, keepdims=True)
-        zgot[2 + m, 0] = (above + inner * scale).astype(BF)
+        for h in range(2):
+            grad = row_sum(1, m, h)
+            xhat, scale = standard(xrow[m, halves[h]].astype(F32))
+            above = grow[m, halves[h]].astype(F32)
+            a = grad * gain_ref[...]
+            inner = a - jnp.mean(a, axis=-1, keepdims=True) - xhat * jnp.mean(a * xhat, axis=-1, keepdims=True)
+            zgot[2 + m, 0, halves[h]] = (above + inner * scale).astype(BF)
+
+            @pl.when(section == 1)
+            def _():
+                onward(1, m, h).start()
+
+            tally[0, 0:1, :] += jnp.sum(grad * xhat, axis=0, keepdims=True)
+            tally[0, 1:2, :] += jnp.sum(grad, axis=0, keepdims=True)
+            tally[0, 2:3, :] += jnp.sum(above, axis=0, keepdims=True)
+
         keep(1, m).start()
-
-        @pl.when(section == 1)
-        def _():
-            onward(1, m).start()
 
     lanes = lax.broadcasted_iota(jnp.int32, (SLOT, 128), 1) % HD
     early = lanes < ROT // 2
@@ -418,9 +450,13 @@
         slope[slot(i)] = (half + 0.5 * v * (1.0 - bent * bent) * (root * (1.0 + 3 * 0.044715 * square))).astype(BF)
 
     def forward_second(i):
-        for at in (0, D // 2):
-            span = slice(at, at + D // 2)
+        for q in range(2):
+            span = slice(q * (D // 2), (q + 1) * (D // 2))
             part[part_at(i), :, span] = dot(hcat[slot(i)], wb[:, span]).astype(BF)
+
+            @pl.when(lax.rem(i, 2) != core)
+            def _():
+                to_pair(0, i, q).start()
 
     def backward_first(i):
         grad_hidden = dot_nt(grads[slot(i)], wb[...])
@@ -456,9 +492,21 @@
             sum_a[0:1, span] += jnp.sum(piece.astype(F32), axis=0, keepdims=True)
 
     def backward_second(i):
-        for at in (0, D // 2):
-            span = slice(at, at + D // 2)
+        other_slot = lax.rem(i, 2) != core
+
+        @pl.when(other_slot)
+        def _():
+            pl.semaphore_wait(pair_free.at[i // 2], 1)
+            for q in range(2):
+                to_pair(0, i, q).wait_send()
+
+        for q in range(2):
+            span = slice(q * (D // 2), (q + 1) * (D // 2))
             part[part_at(i), :, span] = dot_nt(gproj[slot(i)], wa[span, :]).astype(BF)
+
+            @pl.when(other_slot)
+            def _():
+                to_pair(1, i, q).start()
 
     for copy in holds + gives:
         copy.start()
@@ -484,13 +532,13 @@
     def _():
         rows_in[0].wait()
         for m in range(2):
-            spread_own(0, m)
+            spread_own(0, m, False)
 
     @pl.when(section == 1)
     def _():
         rows_in[1].wait()
         for m in range(2):
-            spread_own(1, m)
+            spread_own(1, m, False)
 
     for at in (4, 5):
         holds[at].wait()
@@ -546,13 +594,6 @@
     pass_on_crossed(1)
     settle(1)
 
-    def forward_last(i):
-        forward_second(i)
-
-        @pl.when(lax.rem(i, 2) != core)
-        def _():
-            to_pair(0, i).start()
-
     def finish_forward_all():
         for m in range(2):
             finish_forward(m)
@@ -560,7 +601,7 @@
     @pl.when(section == 0)
     def _():
         def step(i, _):
-            forward_last(i)
+            forward_second(i)
 
             @pl.when(i == 1 + core)
             def _():
@@ -574,17 +615,12 @@
 
         @pl.when(core == 0)
         def _():
-            onward(1, 0).wait_recv()
-            spread_own(1, 0)
+            spread_own(1, 0, True)
             relay(1, 0)
 
     @pl.when(section == 1)
     def _():
-        def arrive(m):
-            onward(0, m).wait_recv()
-            spread_own(0, m)
-
-        arrive(0)
+        spread_own(0, 0, True)
 
         @pl.when(core == 0)
         def _():
@@ -596,7 +632,7 @@
 
             @pl.when((i == 0) & (core == 0))
             def _():
-                arrive(1)
+                spread_own(0, 1, True)
 
             @pl.when((i < 3) & (lax.rem(i, 2) != core))
             def _():
@@ -607,11 +643,11 @@
                 pair_add(0, (i - 1) // 2)
                 aside((i - 1) // 2).start()
 
-            forward_last(i)
+            forward_second(i)
 
             @pl.when((i == 0) & (core == 1))
             def _():
-                arrive(1)
+                spread_own(0, 1, True)
 
             return 0
 
@@ -672,7 +708,7 @@
     b_spans = (pl.ds(0, B_HALF), pl.ds(B_HALF, B_HALF))
 
     def far_piece(way, x_at):
-        source = wa.at[pl.ds(pl.multiple_of(x_at * 256, 256), 256), a_spans[way]]
+        source = far_a.at[x_at, :, a_spans[way]]
         return remote(source, half_a.at[way, x_at], fs.at[way, x_at], fr.at[way, x_at], me.beside(1 - 2 * way))
 
     def far_piece_b(way):
@@ -689,11 +725,15 @@
     def cross_last():
         return remote(a_place(6), xa_in, xs.at[4, 0], xr.at[4, 0], me.across)
 
-    def send_far(x_at):
-        target = pl.ds(pl.multiple_of(x_at * 256, 256), 256)
-        for way, (lo, hi) in enumerate(a_cuts):
-            wa[target, lo:hi] = term_a(far, x_at, way).astype(BF)
-            start(far_piece(way, x_at))
+    def send_far_all():
+        def step(k, _):
+            x_at = (1 - k) * (1 - x) + k * x
+            for way, (lo, hi) in enumerate(a_cuts):
+                far_a[x_at, :, lo:hi] = term_a(far, x_at, way).astype(BF)
+                far_piece(way, x_at).start()
+            return 0
+
+        lax.fori_loop(0, 2, step, 0)
 
     def send_near(way, x_at):
         target = pl.ds(pl.multiple_of((2 + 2 * way + x_at) * 256, 256), 256)
@@ -770,8 +810,7 @@
 
         @pl.when((section == 0) & (i < 3) & jnp.logical_not(own))
         def _():
-            onward(1, (i + 1) // 2).wait_recv()
-            spread_own(1, (i + 1) // 2)
+            spread_own(1, (i + 1) // 2, True)
 
         await_rows(1, i)
         backward_first(i)
@@ -786,6 +825,7 @@
 
         @pl.when((section == 0) & (i == 3))
         def _():
+            send_far_all()
             cross_all()
 
         @pl.when((i >= 1) & jnp.logical_not(own))
@@ -809,17 +849,7 @@
         def _():
             aside(i // 2).wait()
 
-        @pl.when(jnp.logical_not(own))
-        def _():
-            to_pair(0, i).wait_send()
-
         backward_second(i)
-
-        @pl.when(jnp.logical_not(own))
-        def _():
-            pl.semaphore_wait(pair_free.at[i // 2], 1)
-            to_pair(1, i).start()
-
         return 0
 
     lax.fori_loop(0, 4, backward_step, 0)
@@ -831,10 +861,8 @@
             pair_sum(1, 1)
 
         finish_backward(1)
+        send_far_all()
         cross_all()
-
-    send_far(1 - x)
-    send_far(x)
 
     @pl.when((section == 0) & (core == 1))
     def _():
@@ -925,19 +953,24 @@
     for k in range(4):
         for copy in cross(k):
             copy.wait_send()
+    for way in range(2):
+        for x_at in range(2):
+            far_piece(way, x_at).wait_send()
     for back in range(2):
         for m in range(2):
             mine = 2 * m + core
-            for k in range(3):
-                to_z(back, m, mine, k).wait_send()
-            for k in range(4):
-                to_sibling(back, m, mine, k).wait_send()
+            for h in range(2):
+                for k in range(3):
+                    to_z(back, m, mine, k, h).wait_send()
+                for k in range(4):
+                    to_sibling(back, m, mine, k, h).wait_send()
             keep(back, m).wait()
 
         @pl.when(section == back)
         def _():
             for m in range(2):
-                onward(back, m).wait_send()
+                for h in range(2):
+                    onward(back, m, h).wait_send()
 
         @pl.when(section != back)
         def _():
@@ -945,7 +978,8 @@
                 pair_sent(back, m)
 
     for m in range(2):
-        to_pair(1, 2 * m + 1 - core).wait_send()
+        for q in range(2):
+            to_pair(1, 2 * m + 1 - core, q).wait_send()
     for at in range(6):
         staying[at].wait()
         outgoing[at].wait_send()
@@ -1001,6 +1035,7 @@
             pltpu.VMEM((8, 128), jnp.int32),
             pltpu.VMEM((8, 128), jnp.int32),
             pltpu.VMEM((8, A_COLS), F32),
+            pltpu.VMEM((2, 256, A_COLS), BF),
             pltpu.VMEM((2, 2, 256, A_HALF), BF),
             pltpu.VMEM((2, B_HALF, 256), BF),
             pltpu.VMEM((2, 2, 256, A_COLS), BF),
@@ -1016,16 +1051,16 @@
             dma((2, 2, 9)),
             dma((7,)),
             dma((7,)),
-            dma((2, 2, 3)),
-            dma((2, 2, 3)),
-            dma((2, 2, 4)),
-            dma((2, 2, 4)),
-            dma((2, 2)),
-            dma((2, 2)),
-            dma((2, 2, 3)),
-            dma((2, 2, 3)),
-            dma((2, 2)),
-            dma((2, 2)),
+            dma((2, 2, 6)),
+            dma((2, 2, 6)),
+            dma((2, 2, 8)),
+            dma((2, 2, 8)),
+            dma((2, 2, 2)),
+            dma((2, 2, 2)),
+            dma((2, 2, 6)),
+            dma((2, 2, 6)),
+            dma((2, 2, 2)),
+            dma((2, 2, 2)),
             dma((5, 2)),
             dma((5, 2)),
             dma((2, 3)),

time: 360 us -> 337 us (0.936)
  Pallas kernels: 338 us -> 315 us
    pallas_call x1, Pallas kernels: 338 us -> 315 us  [both_layers(): pl.pallas_call(layers_kernel, out_shape=(shape((2, ROWS, D), BF), shape((...]
where the time goes in v4:
time: 337 us; the launch traced here: 331 us
  Pallas kernels  315 us (93%)
  local copies, waits for them, and re-layouts  8.42 us (2%)
  other arithmetic  6.87 us (2%)
    pallas_call x1, Pallas kernels, both_layers(): pl.pallas_call(layers_kernel, out_shape=(shape((2, ROWS, D), BF), shape((...  315 us

profile of v4, /device:TPU:1, one launch (start us, length us, event | category | flops | bytes accessed | tf_op | source)
XLA Modules:
  0.0 331.1 jit_solution(15637889459079671669)
XLA Ops:
  0.6 0.7 broadcast_in_dim.46
  1.3 0.1 broadcast_in_dim.47
  1.4 0.7 broadcast_in_dim.48.mine_ref
  2.1 1.3 copy.35
  3.3 314.8 %both_layers.1 = (bf16[2,64,2048]{2,1,0:T(8,128)(2,1)}, bf16[2,64,2048]{2,1,0:T(8,128)(2,1)}, bf16[3,128,512]{2,1,0:T(8,128)(2,1)}, bf16[128,2048]{1,0:T(8,128)(...) custom-call(bf16[2,64,2048]{2,1,0:T(8,128)(2,1)} %bitcast.34, ...), custom_call_target="tpu_custom_call" | custom-call | tf_op jit(solution)/shard_map/both_layers/pallas_call | solution.py:1002
  318.2 0.0 copy-start
  318.2 1.4 copy.32
  319.6 1.6 fusion
  321.1 0.0 copy-start.3
  321.1 1.6 bitcast_convert_fusion.2
  322.8 0.0 copy-start.2
  322.8 2.0 convert_bitcast_fusion
  324.8 0.0 copy-start.1
  324.8 2.2 bitcast_convert_fusion.1
  327.0 0.0 copy-done
  327.0 1.0 bitcast_convert_fusion
  328.0 0.0 copy-done.3
  328.0 0.6 copy.40
  328.6 0.0 copy-done.2
  328.6 0.8 copy.41
  329.4 0.0 copy-done.1
  329.4 0.8 copy.42
  330.2 0.0 copy-done.4
  330.2 0.6 copy.43
  (1 shorter events, 0.0 us)
Async XLA Ops:
  318.2 8.8 %copy-start = (bf16[2048,128]{1,0:T(8,128)(2,1)S(1)}, bf16[2048,128]{1,0:T(8,128)(2,1)}, u32[]{:S(2)}) copy-start(bf16[2048,128]{1,0:T(8,128)(2,1)} %get-tuple-element.29) | copy-start | bytes 1572868
  321.1 6.9 %copy-start.3 = (f32[1,2048]{1,0:T(1,128)}, f32[1,2048]{1,0:T(1,128)S(1)}, u32[]{:S(2)}) copy-start(f32[1,2048]{1,0:T(1,128)S(1)} %get-tuple-element.98) | copy-start | bytes 24580
  322.8 5.9 %copy-start.2 = (bf16[2,64,2048]{2,1,0:T(8,128)(2,1)S(1)}, bf16[2,64,2048]{2,1,0:T(8,128)(2,1)}, u32[]{:S(2)}) copy-start(bf16[2,64,2048]{2,1,0:T(8,128)(2,1)} %get-tuple-element.21) | copy-start | bytes 1572868
  324.8 4.6 %copy-start.1 = (bf16[2,64,2048]{2,1,0:T(8,128)(2,1)S(1)}, bf16[2,64,2048]{2,1,0:T(8,128)(2,1)}, u32[]{:S(2)}) copy-start(bf16[2,64,2048]{2,1,0:T(8,128)(2,1)} %get-tuple-element.22) | copy-start | bytes 1572868
  327.0 3.2 copy-start.4

commit v5 on v4

--- a/solution.py
+++ b/solution.py
@@ -88,7 +88,7 @@
     x_hbm, cot_hbm, qkv_hbm, up_hbm, ow_hbm, dw_hbm,
     qb_ref, ub_ref, ob_ref, db_ref, gain_ref, shift_ref, mine_ref, cos_ref, sin_ref,
     lo_out, ig_out, gq_out, gu_out, go_out, gd_out, sums_ref, gqb_ref, gub_ref, aside_out,
-    wa, wb, normed, grads, qkv, hcat, slope, probs, gproj, part, got, zgot, xrow, grow, ctab, stab, split, theirs, bias,
+    wa, wb, normed, grads, qkv, hcat, slope, probs, gproj, part, got, zgot, xrow, grow, ctab, stab, split, ours, theirs, bias,
     far_a, half_a, half_b, got_a, got_b, xa_in, sum_a, tally, came,
     own_sem, x_send, x_recv, y_send, y_recv, sib_send, sib_recv,
     agz_s, agz_r, ags_s, ags_r, par_s, par_r, rsz_s, rsz_r, sec_s, sec_r,
@@ -134,7 +134,7 @@
         remote(source, target, sib_send.at[at], sib_recv.at[at], me.sibling)
         for at, (source, target) in enumerate(blocks(other, 1 - core))
     ]
-    tell = remote(mine_ref, theirs, sib_send.at[6], sib_recv.at[6], me.sibling)
+    tell = remote(ours, theirs, sib_send.at[6], sib_recv.at[6], me.sibling)
     rows_in = [
         pltpu.make_async_copy(x_hbm, xrow, own_sem.at[6]),
         pltpu.make_async_copy(cot_hbm, grow, own_sem.at[6]),
@@ -510,6 +510,9 @@
 
     for copy in holds + gives:
         copy.start()
+    ours[...] = jnp.zeros_like(ours)
+    for m in range(2):
+        ours[m : m + 1, :] = jnp.broadcast_to(mine_ref[0:1, m : m + 1], (1, 128))
     tell.start()
 
     @pl.when(section == 0)
@@ -545,12 +548,12 @@
         takes[at].wait_recv()
     for at in range(3):
         bias[0:1, at * MIX : (at + 1) * MIX] = jnp.where(
-            core == 0, qb_ref[at : at + 1, 0:MIX], qb_ref[at : at + 1, MIX : 2 * MIX]
+            core == 0, qb_ref[at, 0:1, 0:MIX], qb_ref[at, 0:1, MIX : 2 * MIX]
         )
     bias[0:1, QKV:A_COLS] = jnp.where(core == 0, ub_ref[0:1, 0:UP], ub_ref[0:1, UP : 2 * UP])
     tell.wait_recv()
     for i in range(4):
-        at = jnp.where(core == i % 2, mine_ref[i // 2 : i // 2 + 1, :], theirs[i // 2 : i // 2 + 1, :])
+        at = jnp.where(core == i % 2, ours[i // 2 : i // 2 + 1, :], theirs[i // 2 : i // 2 + 1, :])
         split[i : i + 1, :] = at
         here = places == at
         ctab[i : i + 1, :] = jnp.sum(jnp.where(here, cos_ref[...], 0.0), axis=0, keepdims=True)
@@ -630,7 +633,7 @@
             await_rows(0, i)
             forward_first(i)
 
-            @pl.when((i == 0) & (core == 0))
+            @pl.when(i == core)
             def _():
                 spread_own(0, 1, True)
 
@@ -644,17 +647,12 @@
                 aside((i - 1) // 2).start()
 
             forward_second(i)
-
-            @pl.when((i == 0) & (core == 1))
-            def _():
-                spread_own(0, 1, True)
-
             return 0
 
         lax.fori_loop(0, 4, step, 0)
 
     def turn_of(k):
-        return lax.rem(y + 2 - k + 4, 4)
+        return lax.rem(y + 2 + 3 * k + 3 * (k // 2) + 2 * (k // 3), 4)
 
     a_cuts = ((0, A_HALF), (A_HALF, A_COLS))
     b_cuts = ((0, B_HALF), (B_HALF, B_COLS))
@@ -747,17 +745,21 @@
         start(near_piece(way, x_at))
 
     def send_far_b():
-        crossed(0)
         for way, (lo, hi) in enumerate(b_cuts):
-            wb[lo:hi, 0:256] = (term_b(far, x, way) + from_across(0, way)).astype(BF)
+            total = term_b(far, x, way)
+            if way == 0:
+                crossed(0)
+            wb[lo:hi, 0:256] = (total + from_across(0, way)).astype(BF)
             start(far_piece_b(way))
 
     def send_near_b(way):
-        crossed(1 + 2 * way)
         span = slice((1 + way) * 256, (2 + way) * 256)
         for half in (1 - way, way):
             lo, hi = b_cuts[half]
-            total = term_b(me.turn(1 - 2 * way), x, half) + from_across(1 + 2 * way, half)
+            total = term_b(me.turn(1 - 2 * way), x, half)
+            if half != way:
+                crossed(1 + way)
+            total = total + from_across(1 + way, half)
             if half == way:
                 far_piece_b(way).wait_recv()
                 total = total + half_b[way].astype(F32)
@@ -773,19 +775,22 @@
                 total = total + got_a[way, x_at, :, lo:hi].astype(F32)
             wa[at * 256 : (at + 1) * 256, lo:hi] = total.astype(BF)
 
+    def begun_b(at):
+        crossed(3)
+        for half, (lo, hi) in enumerate(b_cuts):
+            wb[lo:hi, at * 256 : (at + 1) * 256] = (term_b(y, x, half) + from_across(3, half)).astype(BF)
+
     def arrived_b(at):
-        crossed(2)
-        for half, (lo, hi) in enumerate(b_cuts):
-            total = term_b(y, x, half) + from_across(2, half)
-            for way in (0, 1):
-                if half == 0:
-                    near_piece_b(way).wait_recv()
-                total = total + got_b[way, lo:hi].astype(F32)
-            wb[lo:hi, at * 256 : (at + 1) * 256] = total.astype(BF)
+        span = slice(at * 256, (at + 1) * 256)
+        total = wb[:, span].astype(F32)
+        for way in (0, 1):
+            near_piece_b(way).wait_recv()
+            total = total + got_b[way].astype(F32)
+        wb[:, span] = total.astype(BF)
 
     near_z = {"tensor": z + 1 - 2 * lax.rem(z, 2)}
     near_y = {"dp": me.at(y + 1 - 2 * lax.rem(y, 2), x, core)}
-    partners = (me.across, near_y, me.beside(2), near_z, me.z_peer(2), me.sibling)
+    partners = (near_z, me.z_peer(2), me.sibling, me.across, near_y, me.beside(2))
 
     def exchange(step):
         return remote(tally.at[step], came.at[step], ts.at[step], tr.at[step], partners[step])
@@ -794,10 +799,12 @@
         exchange(step).wait_recv()
         total = tally[step] + came[step]
         if step < 3:
-            tally[step + 1] = total
-        else:
             tally[step + 1, 0:3] = total[0:3]
             tally[step + 1, 3:8] = tally[step, 3:8]
+            if step == 2:
+                tally[step + 1, 4:5] = came[step, 3:4]
+        else:
+            tally[step + 1] = total
         if step < 5:
             start(exchange(step + 1))
 
@@ -808,14 +815,18 @@
     def backward_step(i, _):
         own = lax.rem(i, 2) == core
 
-        @pl.when((section == 0) & (i < 3) & jnp.logical_not(own))
-        def _():
-            spread_own(1, (i + 1) // 2, True)
+        @pl.when((section == 0) & (i + core == 1))
+        def _():
+            spread_own(1, 1 - core, True)
 
         await_rows(1, i)
         backward_first(i)
 
-        @pl.when((section == 0) & (i < 3) & jnp.logical_not(own))
+        @pl.when((section == 0) & (i == 1) & (core == 1))
+        def _():
+            spread_own(1, 1, True)
+
+        @pl.when((section == 0) & (lax.rem(i, 2) == 0) & (i < 3) & jnp.logical_not(own))
         def _():
             relay(1, i + 1)
 
@@ -828,11 +839,11 @@
             send_far_all()
             cross_all()
 
-        @pl.when((i >= 1) & jnp.logical_not(own))
+        @pl.when((section == 1) & (i >= 1) & jnp.logical_not(own))
         def _():
             pair_sum(1, (i - 1) // 2)
 
-        @pl.when((i >= 2) & own)
+        @pl.when((section == 1) & (i >= 2) & own)
         def _():
             finish_backward(0)
 
@@ -850,6 +861,11 @@
             aside(i // 2).wait()
 
         backward_second(i)
+
+        @pl.when((section == 0) & (i == 1) & jnp.logical_not(own))
+        def _():
+            relay(1, 2)
+
         return 0
 
     lax.fori_loop(0, 4, backward_step, 0)
@@ -864,48 +880,45 @@
         send_far_all()
         cross_all()
 
-    @pl.when((section == 0) & (core == 1))
+    @pl.when(section == 0)
     def _():
-        pair_sum(1, 1)
+        for m in range(2):
+            pair_sum(1, m)
 
     @pl.when(section == 1)
     def _():
         for m in range(2):
             pair_sent(1, m)
             back_again(m).start()
-
-    send_far_b()
-
-    @pl.when(section == 1)
-    def _():
         for m in range(2):
             back_again(m).wait()
             pair_spread(0, m)
 
-    for way in (0, 1):
-        send_near(way, 1 - x)
+    send_far_b()
+    for x_at in (1 - x, x):
+        for way in (0, 1):
+            send_near(way, x_at)
 
     @pl.when(section == 0)
     def _():
-        finish_backward(1)
-
-    tally[0, 3:4, 0:A_COLS] = sum_a[0:1]
-    start(exchange(0))
-    for way in (0, 1):
-        send_near(way, x)
-    fold(0)
-    for way in (0, 1):
-        send_near_b(way)
-    fold(1)
+        for m in range(2):
+            finish_backward(m)
 
     @pl.when(section == 1)
     def _():
         finish_forward_all()
 
+    tally[0, 3:4, 0:A_COLS] = sum_a[0:1]
+    start(exchange(0))
+    send_near_b(0)
+    fold(0)
+    fold(1)
+    send_near_b(1)
+    fold(2)
     arrived_a(1 - x, 6)
     start(cross_last())
-    fold(2)
-    arrived_b(3)
+    arrived_a(x, 7)
+    begun_b(3)
     fold(3)
 
     def result(half, peer, at):
@@ -927,26 +940,26 @@
 
     outgoing, staying = result(1 - core, True, core), result(core, False, core)
     incoming = result(1 - core, True, 1 - core)
-    for at in (4, 5):
-        outgoing[at].start()
-        staying[at].start()
-    fold(4)
-    arrived_a(x, 7)
-    fold(5)
-    sums_ref[...] = tally[6]
-    for at in range(3):
-        span = slice(at * MIX, (at + 1) * MIX)
-        ours, others = tally[6, 3:4, span], came[5, 3:4, span]
-        gqb_ref[at : at + 1, 0:MIX] = jnp.where(core == 0, ours, others)
-        gqb_ref[at : at + 1, MIX : 2 * MIX] = jnp.where(core == 0, others, ours)
-    ours, others = tally[6, 3:4, QKV:A_COLS], came[5, 3:4, QKV:A_COLS]
-    gub_ref[0:1, 0:UP] = jnp.where(core == 0, ours, others)
-    gub_ref[0:1, UP : 2 * UP] = jnp.where(core == 0, others, ours)
     cross_last().wait_recv()
     wa[7 * 256 : 8 * 256] = (wa[7 * 256 : 8 * 256].astype(F32) + xa_in[...].astype(F32)).astype(BF)
     for at in range(4):
         outgoing[at].start()
         staying[at].start()
+    fold(4)
+    arrived_b(3)
+    for at in (4, 5):
+        outgoing[at].start()
+        staying[at].start()
+    fold(5)
+    sums_ref[...] = tally[6]
+    for at in range(3):
+        span = slice(at * MIX, (at + 1) * MIX)
+        ours_a, others_a = tally[6, 3:4, span], tally[6, 4:5, span]
+        gqb_ref[at : at + 1, 0:MIX] = jnp.where(core == 0, ours_a, others_a)
+        gqb_ref[at : at + 1, MIX : 2 * MIX] = jnp.where(core == 0, others_a, ours_a)
+    ours_a, others_a = tally[6, 3:4, QKV:A_COLS], tally[6, 4:5, QKV:A_COLS]
+    gub_ref[0:1, 0:UP] = jnp.where(core == 0, ours_a, others_a)
+    gub_ref[0:1, UP : 2 * UP] = jnp.where(core == 0, others_a, ours_a)
 
     for copy in sent + gives + [tell]:
         copy.wait_send()
@@ -1032,6 +1045,7 @@
             pltpu.VMEM((2, ROWS, D), BF),
             pltpu.VMEM((8, 128), F32),
             pltpu.VMEM((8, 128), F32),
+            pltpu.VMEM((8, 128), jnp.int32),
             pltpu.VMEM((8, 128), jnp.int32),
             pltpu.VMEM((8, 128), jnp.int32),
             pltpu.VMEM((8, A_COLS), F32),
@@ -1087,6 +1101,51 @@
     )
 
 
+def widen_kernel(lo, ig, gq, gu, go, gd, sums, gqb, gub, *outs):
+    lo_out, ig_out, gq_out, gu_out, go_out, gd_out, gain, shift, out_b, down_b, qkv_b, up_b = outs
+    lo_out[...] = lo[...]
+    ig_out[...] = ig[...]
+    gq_out[...] = gq[...].astype(F32)
+    gu_out[...] = gu[...].astype(F32)
+    go_out[...] = go[...].astype(F32)
+    gd_out[...] = gd[...].astype(F32)
+    gain[...] = sums[0:1]
+    shift[...] = sums[1:2]
+    out_b[...] = sums[2:3]
+    down_b[...] = sums[2:3]
+    for k in range(3):
+        qkv_b[k] = gqb[k : k + 1]
+    up_b[...] = gub[...]
+
+
+def widened(lo, ig, gq, gu, go, gd, sums, gqb, gub):
+    steps = 4
+    shape = jax.ShapeDtypeStruct
+
+    def cut(whole, dim):
+        block = tuple(size // steps if at == dim else size for at, size in enumerate(whole))
+        return pl.BlockSpec(block, lambda i: tuple(i if at == dim else 0 for at in range(len(whole))))
+
+    def same(whole):
+        return pl.BlockSpec(whole, lambda i: (0,) * len(whole))
+
+    large = [cut(lo.shape, 1), cut(ig.shape, 1), cut(gq.shape, 1), cut(gu.shape, 0), cut(go.shape, 0), cut(gd.shape, 0)]
+    small = [(1, D)] * 4 + [(3, 1, 2 * MIX), (1, 2 * UP)]
+    return pl.pallas_call(
+        widen_kernel,
+        grid=(steps,),
+        out_shape=(
+            [shape(lo.shape, BF), shape(ig.shape, BF)]
+            + [shape(each.shape, F32) for each in (gq, gu, go, gd)]
+            + [shape(each, F32) for each in small]
+        ),
+        in_specs=large + [same(sums.shape), same(gqb.shape), same(gub.shape)],
+        out_specs=large + [same(each) for each in small],
+        compiler_params=pltpu.CompilerParams(vmem_limit_bytes=VMEM_LIMIT),
+        name="widened",
+    )(lo, ig, gq, gu, go, gd, sums, gqb, gub)
+
+
 def shards(
     inputs,
     cotangent,
@@ -1102,35 +1161,37 @@
     ln_gain,
     ln_bias,
 ):
-    mine = jnp.broadcast_to(doc_split[None], (4, 2, 128)).reshape(8, 128)
-    layer_out, input_grad, grad_qkv, grad_up, grad_out, grad_down, sums, grad_qkv_bias, grad_up_bias, _ = both_layers(
+    results = both_layers(
         inputs[:, 0],
         cotangent[:, 0],
         qkv_weight[0].transpose(1, 0, 2),
         fc1_weight[0],
         out_weight[0],
         fc2_weight[0],
-        qkv_bias[0],
+        qkv_bias[0][:, None, :],
         fc1_bias,
         out_bias,
         fc2_bias,
         ln_gain,
         ln_bias,
-        mine,
+        doc_split.reshape(1, 2),
+    )
+    layer_out, input_grad, grad_qkv, grad_up, grad_out, grad_down, gain, shift, out_b, down_b, qkv_b, up_b = widened(
+        *results[:9]
     )
     return (
         layer_out[None, :, None],
         input_grad[None, :, None],
-        grad_qkv.transpose(1, 0, 2).astype(F32)[None],
-        grad_qkv_bias[None],
-        grad_out.astype(F32)[None],
-        sums[2:3],
-        grad_up.astype(F32)[None],
-        grad_up_bias,
-        grad_down.astype(F32)[None],
-        sums[2:3],
-        sums[0:1],
-        sums[1:2],
+        grad_qkv.transpose(1, 0, 2)[None],
+        qkv_b.transpose(1, 0, 2),
+        grad_out[None],
+        out_b,
+        grad_up[None],
+        up_b,
+        grad_down[None],
+        down_b,
+        gain,
+        shift,
     )
 
 

time: 337 us -> 313 us (0.929)
  Pallas kernels: 315 us -> 306 us
  local copies, waits for them, and re-layouts: 8.42 us -> 0 us
  other arithmetic: 6.87 us -> 0 us
    pallas_call x1, Pallas kernels: 315 us -> 301 us  [both_layers(): pl.pallas_call(layers_kernel, out_shape=(shape((2, ROWS, D), BF), shape((...]
    broadcast_in_dim x4 -> x0, other arithmetic: 6.87 us -> none  [the longest x1 2.18 us: shards(): grad_up.astype(F32)[None]]
    unnamed x16 -> x0, local copies, waits for them, and re-layouts: 5.45 us -> none
    pallas_call x0 -> x1, Pallas kernels: none -> 4.53 us  [widened(): pl.pallas_call(widen_kernel, grid=(steps,), out_shape=[shape(lo.shape, BF...]
where the time goes in v5:
time: 313 us; the launch traced here: 307 us
  Pallas kernels  306 us (98%)
    pallas_call x1, Pallas kernels, both_layers(): pl.pallas_call(layers_kernel, out_shape=(shape((2, ROWS, D), BF), shape((...  301 us

profile of v5, /device:TPU:1, one launch (start us, length us, event | category | flops | bytes accessed | tf_op | source)
XLA Modules:
  0.0 306.8 jit_solution(9436532645173257562)
XLA Ops:
  0.6 301.2 %both_layers.1 = (bf16[2,64,2048]{2,1,0:T(8,128)(2,1)}, bf16[2,64,2048]{2,1,0:T(8,128)(2,1)}, bf16[3,128,512]{2,1,0:T(8,128)(2,1)}, bf16[128,2048]{1,0:T(8,128)(...) custom-call(bf16[2,64,2048]{2,1,0:T(8,128)(2,1)} %bitcast.23, ...), custom_call_target="tpu_custom_call" | custom-call | tf_op jit(solution)/shard_map/both_layers/pallas_call | solution.py:1015
  301.8 4.5 %widened.1 = (bf16[2,64,2048]{2,1,0:T(8,128)(2,1)}, bf16[2,64,2048]{2,1,0:T(8,128)(2,1)}, f32[3,128,512]{2,1,0:T(8,128)}, f32[128,2048]{1,0:T(8,128)}, f32[512,1...) custom-call(bf16[2,64,2048]{2,1,0:T(8,128)(2,1)} %get-tuple-element., ...), custom_call_target="tpu_custom_call" | custom-call | tf_op jit(solution)/shard_map/widened/pallas_call | solution.py:1134
